TPU v7x, 32 devices: a whole 2x2x4 slice. The times are simulated.
32 devices in a mesh: dp: 4 (over y, x), fsdp: 8 (over z, core).
Axes of the slice: x: 2, y: 2, z: 4, core: 2. Of those that a mesh axis runs over, the one named last changes fastest.
Arguments:
- enc_input: bfloat16 [8192, 768], P(('dp', 'fsdp')), may hold values from -6 to 6
- enc_segments: int32 [32, 256], P(('dp', 'fsdp')), may hold values from 0 to 5, never falling along the last dimension, each value on 1 to 49 neighbouring positions
- dec_segments: int32 [32, 1024], P(('dp', 'fsdp')), may hold values from 0 to 3, never falling along the last dimension, each value on 1 to 392 neighbouring positions
- block_order: int32 [4, 64], P('dp', 'fsdp'), may hold values from 0 to 63, each once within a row
- dec_cotangent: bfloat16 [32768, 512], P(('dp', 'fsdp')), may hold values from -6 to 6
- enc_qkv: bfloat16 [768, 2304], P(('dp', 'fsdp')), may hold values from -0.21875 to 0.21875
- enc_proj: bfloat16 [768, 768], P(('dp', 'fsdp')), may hold values from -1.5 to 1.5
- enc_fc1: bfloat16 [768, 3072], P(('dp', 'fsdp')), may hold values from -0.21875 to 0.21875
- enc_fc2: bfloat16 [3072, 768], P(('dp', 'fsdp')), may hold values from -0.109375 to 0.109375
- enc_gains: bfloat16 [3, 768], P(None, ('dp', 'fsdp')), may hold values from 0.5 to 1.5
- enc_biases: bfloat16 [7, 768], P(None, ('dp', 'fsdp')), may hold values from -1.75 to 1.75
- enc_fc1_bias: bfloat16 [3072], P(('dp', 'fsdp')), may hold values from -1.75 to 1.75
- embed: bfloat16 [768, 512], P(('dp', 'fsdp')), may hold values from -0.21875 to 0.21875
- mask_token: bfloat16 [512], P(('dp', 'fsdp')), may hold values from -6 to 6
- dec_qkv: bfloat16 [512, 1536], P(('dp', 'fsdp')), may hold values from -0.25 to 0.25
- dec_proj: bfloat16 [512, 512], P(('dp', 'fsdp')), may hold values from -6 to 6
- dec_fc1: bfloat16 [512, 2048], P(('dp', 'fsdp')), may hold values from -0.25 to 0.25
- dec_fc2: bfloat16 [2048, 512], P(('dp', 'fsdp')), may hold values from -0.125 to 0.125
- dec_gains: bfloat16 [2, 512], P(None, ('dp', 'fsdp')), may hold values from 0.5 to 1.5
- dec_biases: bfloat16 [6, 512], P(None, ('dp', 'fsdp')), may hold values from -1.75 to 1.75
- dec_fc1_bias: bfloat16 [2048], P(('dp', 'fsdp')), may hold values from -1.75 to 1.75
- dec_fc2_bias: bfloat16 [512], P(('dp', 'fsdp')), may hold values from -1.75 to 1.75
Outputs:
- dec_output: bfloat16 [32768, 512], P(('dp', 'fsdp'))
- enc_input_grad: bfloat16 [8192, 768], P(('dp', 'fsdp'))
- enc_qkv_grad: float32 [768, 2304], P(('dp', 'fsdp'))
- enc_proj_grad: float32 [768, 768], P(('dp', 'fsdp'))
- enc_fc1_grad: float32 [768, 3072], P(('dp', 'fsdp'))
- enc_fc2_grad: float32 [3072, 768], P(('dp', 'fsdp'))
- enc_gains_grad: float32 [3, 768], P(None, ('dp', 'fsdp'))
- enc_biases_grad: float32 [7, 768], P(None, ('dp', 'fsdp'))
- enc_fc1_bias_grad: float32 [3072], P(('dp', 'fsdp'))
- embed_grad: float32 [768, 512], P(('dp', 'fsdp'))
- mask_token_grad: float32 [512], P(('dp', 'fsdp'))
- dec_qkv_grad: float32 [512, 1536], P(('dp', 'fsdp'))
- dec_proj_grad: float32 [512, 512], P(('dp', 'fsdp'))
- dec_fc1_grad: float32 [512, 2048], P(('dp', 'fsdp'))
- dec_fc2_grad: float32 [2048, 512], P(('dp', 'fsdp'))
- dec_gains_grad: float32 [2, 512], P(None, ('dp', 'fsdp'))
- dec_biases_grad: float32 [6, 512], P(None, ('dp', 'fsdp'))
- dec_fc1_bias_grad: float32 [2048], P(('dp', 'fsdp'))
- dec_fc2_bias_grad: float32 [512], P(('dp', 'fsdp'))
Inputs may be any that keep to these rules, and one draw needn't show every extreme that they name: `enc_segments`: within each row of packed sequence, ids never fall; each image has at most 49 rows. `dec_segments`: within each device's row, ids never fall; each decoder sequence has at most 392 rows. `block_order`: each row is a permutation; values below 16 name an encoder block of the same dp index, the others mark mask blocks.
All inputs are finite; a program needn't handle non-finite values.
Results may differ from a plain program's by a relative error of at most 0.02.
Values may be sent and summed in bfloat16 or wider, within the bound.
No kernel may reach another device: no remote copies, remote signals or barrier semaphores. Data moves between devices by JAX's collectives and lax.ppermute only.
A program may use at most 192 MiB of HBM per device.

v0:
```python
import functools
import math

import jax
import jax.numpy as jnp
from jax import lax
from jax.experimental import pallas as pl
from jax.experimental.pallas import tpu as pltpu
from jax.sharding import PartitionSpec as P

HDIM = 64
DHDIM = 32
BLOCK = 128
LANES = 128
TILE = 256
SPAN = 128
GROUP = 256
EPSILON = 1e-06
NEGATIVE = -1e30
LOG2E = math.log2(math.e)
AXES = ("dp", "fsdp")
F32 = jnp.float32
LOW = jnp.bfloat16
PARAMS = pltpu.CompilerParams(vmem_limit_bytes=56 * 1024 * 1024)


def mm(left, right):
    return jnp.dot(left, right, preferred_element_type=F32)


def mm_tn(left, right):
    return lax.dot_general(left, right, (((0,), (0,)), ((), ())), preferred_element_type=F32)


def mm_nt(left, right):
    return lax.dot_general(left, right, (((1,), (1,)), ((), ())), preferred_element_type=F32)


def col_sum(values):
    return jnp.sum(values, axis=0, keepdims=True)


def norm_parts(values):
    centred = values - jnp.mean(values, axis=-1, keepdims=True)
    variance = jnp.mean(centred * centred, axis=-1, keepdims=True)
    scale = lax.rsqrt(variance + EPSILON)
    return centred * scale, scale


def norm_back(grad, unit, scale, gain):
    inner = grad * gain
    mean_inner = jnp.mean(inner, axis=-1, keepdims=True)
    mean_cross = jnp.mean(inner * unit, axis=-1, keepdims=True)
    return scale * (inner - mean_inner - unit * mean_cross)


def gelu_parts(hidden):
    cdf = 0.5 + 0.5 * lax.erf(hidden * (0.5**0.5))
    density = jnp.exp(hidden * hidden * -0.5) * (1.0 / math.sqrt(2.0 * math.pi))
    return hidden * cdf, cdf + hidden * density


CHEAP = pl.CostEstimate(flops=1 << 20, bytes_accessed=1 << 16, transcendentals=0)


def full(shape):
    return pl.BlockSpec(shape, lambda *_: (0,) * len(shape))


def at_col(rows, cols, index):
    return pl.BlockSpec((rows, cols), lambda *_: (0, index))


def shape(dims, kind):
    return jax.ShapeDtypeStruct(dims, kind)


def lane_mask(head, head_dim, kind):
    lane = lax.broadcasted_iota(jnp.int32, (1, GROUP), 1)
    inside = (lane >= head * head_dim) & (lane < (head + 1) * head_dim)
    return inside.astype(F32).astype(kind)


def stack_heads(stacked, index, rows, head_dim):
    count = rows.shape[0]
    for h in range(GROUP // head_dim):
        stacked[index, h * count : (h + 1) * count, :] = rows * lane_mask(h, head_dim, LOW)


def tile_range(seg_ref, start, size, other, count):
    first, last = seg_ref[0, start], seg_ref[0, start + size - 1]
    low, high = jnp.int32(0), jnp.int32(count)
    for tile in range(count):
        low += (seg_ref[0, tile * other + other - 1] < first).astype(jnp.int32)
        high -= (seg_ref[0, tile * other] > last).astype(jnp.int32)
    return low, high


def attend_kernel(
    head_dim,
    tiles,
    seg_ref,
    q_ref,
    k_ref,
    v_ref,
    row_ref,
    col_ref,
    out_ref,
    inv_ref,
    exp_ref,
    km,
    vt,
    held,
    acc,
    inverse,
    top,
    tot,
):
    heads = GROUP // head_dim
    here = pl.program_id(1)
    factor = head_dim ** (-0.5) * LOG2E

    @pl.when(here == 0)
    def _():
        for u in range(tiles):
            rows = slice(u * SPAN, (u + 1) * SPAN)
            vt[u] = v_ref[rows, :].astype(F32).T.astype(LOW)
            stack_heads(km, u, k_ref[rows, :], head_dim)

    acc[...] = jnp.zeros_like(acc)
    top[...] = jnp.full_like(top, NEGATIVE)
    tot[...] = jnp.zeros_like(tot)
    query = q_ref[...]
    row = row_ref[...]

    def score(u, carry):
        start = pl.multiple_of(u * SPAN, SPAN)
        same = col_ref[pl.ds(start, SPAN), :] == row
        every = mm_nt(km[u], query)
        for h in range(heads):
            scores = jnp.where(same, every[h * SPAN : (h + 1) * SPAN, :], NEGATIVE)
            held[u, h] = scores
            top[h : h + 1, :] = jnp.maximum(
                top[h : h + 1, :], jnp.max(scores, axis=0, keepdims=True)
            )
        return carry

    def mix(u, carry):
        for h in range(heads):
            weights = jnp.exp2((held[u, h] - top[h : h + 1, :]) * factor)
            tot[h : h + 1, :] += col_sum(weights)
            span = slice(h * head_dim, (h + 1) * head_dim)
            weights = weights.astype(LOW)
            exp_ref[0, 0, u, :, h * TILE : (h + 1) * TILE] = weights
            acc[span, :] += mm(vt[u, span, :], weights)
        return carry

    low, high = tile_range(seg_ref, here * TILE, TILE, SPAN, tiles)
    lax.fori_loop(low, high, score, 0)
    lax.fori_loop(low, high, mix, 0)
    for h in range(heads):
        span = slice(h * head_dim, (h + 1) * head_dim)
        inverse[span, :] = jnp.broadcast_to(1.0 / tot[h : h + 1, :], (head_dim, TILE))
    out_ref[...] = (acc[...] * inverse[...]).T.astype(LOW)
    inv_ref[...] = inverse[...].T


def attend(qkv, segments, seg_col, head_dim):
    rows, width = qkv.shape[0], qkv.shape[1] // 3
    groups, steps, tiles, heads = width // GROUP, rows // TILE, rows // SPAN, GROUP // head_dim
    return pl.pallas_call(
        functools.partial(attend_kernel, head_dim, tiles),
        grid_spec=pltpu.PrefetchScalarGridSpec(
            num_scalar_prefetch=1,
            grid=(groups, steps),
            in_specs=[
                pl.BlockSpec((TILE, GROUP), lambda g, t, s: (t, g)),
                pl.BlockSpec((rows, GROUP), lambda g, t, s: (0, groups + g)),
                pl.BlockSpec((rows, GROUP), lambda g, t, s: (0, 2 * groups + g)),
                pl.BlockSpec((1, TILE), lambda g, t, s: (0, t)),
                pl.BlockSpec((rows, 1), lambda g, t, s: (0, 0)),
            ],
            out_specs=[
                pl.BlockSpec((TILE, GROUP), lambda g, t, s: (t, g)),
                pl.BlockSpec((TILE, GROUP), lambda g, t, s: (t, g)),
                pl.BlockSpec((1, 1, tiles, SPAN, heads * TILE), lambda g, t, s: (g, t, 0, 0, 0)),
            ],
            scratch_shapes=[
                pltpu.VMEM((tiles, heads * SPAN, GROUP), LOW),
                pltpu.VMEM((tiles, GROUP, SPAN), LOW),
                pltpu.VMEM((tiles, heads, SPAN, TILE), F32),
                pltpu.VMEM((GROUP, TILE), F32),
                pltpu.VMEM((GROUP, TILE), F32),
                pltpu.VMEM((8, TILE), F32),
                pltpu.VMEM((8, TILE), F32),
            ],
        ),
        out_shape=[
            shape((rows, width), LOW),
            shape((rows, width), F32),
            shape((groups, steps, tiles, SPAN, heads * TILE), LOW),
        ],
        compiler_params=PARAMS,
        cost_estimate=CHEAP,
        name="attend",
    )(segments, qkv, qkv, qkv, segments, seg_col)


def attend_back_kernel(
    head_dim,
    tiles,
    seg_ref,
    q_ref,
    k_ref,
    v_ref,
    o_ref,
    g_ref,
    exp_ref,
    dq_ref,
    dk_ref,
    dv_ref,
    kt,
    vm,
    qm,
    gm,
    dqt,
    delta,
    dk_acc,
    dv_acc,
):
    heads = GROUP // head_dim
    here = pl.program_id(1)
    scale = head_dim ** (-0.5)

    @pl.when(here == 0)
    def _():
        dk_acc[...] = jnp.zeros_like(dk_acc)
        dv_acc[...] = jnp.zeros_like(dv_acc)
        for u in range(tiles):
            rows = slice(u * SPAN, (u + 1) * SPAN)
            kt[u] = k_ref[rows, :].astype(F32).T.astype(LOW)
            stack_heads(vm, u, v_ref[rows, :], head_dim)

    grads = g_ref[...]
    both = (grads.astype(F32) * o_ref[...].astype(F32)).T
    for h in range(heads):
        delta[h : h + 1, :] = col_sum(both[h * head_dim : (h + 1) * head_dim, :])
    stack_heads(qm, 0, q_ref[...], head_dim)
    stack_heads(gm, 0, grads, head_dim)
    dqt[...] = jnp.zeros_like(dqt)

    def step(u, carry):
        rows = pl.ds(pl.multiple_of(u * SPAN, SPAN), SPAN)
        every = mm_nt(vm[u], grads)
        dv_acc[rows, :] += mm(exp_ref[0, 0, u], gm[0])
        pieces = []
        for h in range(heads):
            grad_probs = every[h * SPAN : (h + 1) * SPAN, :] - delta[h : h + 1, :]
            weights = exp_ref[0, 0, u, :, h * TILE : (h + 1) * TILE]
            pieces.append((weights.astype(F32) * grad_probs).astype(LOW))
        for h in range(heads):
            span = slice(h * head_dim, (h + 1) * head_dim)
            dqt[span, :] += mm(kt[u, span, :], pieces[h])
        dk_acc[rows, :] += mm(jnp.concatenate(pieces, axis=1), qm[0])
        return carry

    low, high = tile_range(seg_ref, here * TILE, TILE, SPAN, tiles)
    lax.fori_loop(low, high, step, 0)
    dq_ref[...] = (dqt[...] * scale).T.astype(LOW)

    @pl.when(here == pl.num_programs(1) - 1)
    def _():
        dk_ref[...] = (dk_acc[...] * scale).astype(LOW)
        dv_ref[...] = dv_acc[...].astype(LOW)


def attend_back(qkv, attended, grad, weights, segments, head_dim):
    rows, width = attended.shape
    groups, steps, tiles, heads = width // GROUP, rows // TILE, rows // SPAN, GROUP // head_dim
    whole = pl.BlockSpec((rows, GROUP), lambda g, t, s: (0, g))
    piece = pl.BlockSpec((TILE, GROUP), lambda g, t, s: (t, g))
    return pl.pallas_call(
        functools.partial(attend_back_kernel, head_dim, tiles),
        grid_spec=pltpu.PrefetchScalarGridSpec(
            num_scalar_prefetch=1,
            grid=(groups, steps),
            in_specs=[
                piece,
                pl.BlockSpec((rows, GROUP), lambda g, t, s: (0, groups + g)),
                pl.BlockSpec((rows, GROUP), lambda g, t, s: (0, 2 * groups + g)),
                piece,
                piece,
                pl.BlockSpec((1, 1, tiles, SPAN, heads * TILE), lambda g, t, s: (g, t, 0, 0, 0)),
            ],
            out_specs=[piece, whole, whole],
            scratch_shapes=[
                pltpu.VMEM((tiles, GROUP, SPAN), LOW),
                pltpu.VMEM((tiles, heads * SPAN, GROUP), LOW),
                pltpu.VMEM((1, heads * TILE, GROUP), LOW),
                pltpu.VMEM((1, heads * TILE, GROUP), LOW),
                pltpu.VMEM((GROUP, TILE), F32),
                pltpu.VMEM((8, TILE), F32),
                pltpu.VMEM((rows, GROUP), F32),
                pltpu.VMEM((rows, GROUP), F32),
            ],
        ),
        out_shape=[shape((rows, width), LOW)] * 3,
        compiler_params=PARAMS,
        cost_estimate=CHEAP,
        name="attend_back",
    )(segments, qkv, qkv, qkv, attended, grad, weights)


def pack_kernel(up_ref, down_ref, dup_ref, ddown_ref, out_ref, dout_ref):
    for up, down, out in ((up_ref, down_ref, out_ref), (dup_ref, ddown_ref, dout_ref)):
        rows, cols = up.shape
        out[:, :cols] = up[...]
        wide = down[...].astype(F32)
        width = down.shape[1]
        for part in range(4):
            piece = wide[part * rows : (part + 1) * rows, :].astype(LOW)
            out[:, cols + part * width : cols + (part + 1) * width] = piece


def pack_shards(*shards):
    outs = [shape((w.shape[0], 2 * w.shape[1]), LOW) for w in shards[::2]]
    return pl.pallas_call(
        pack_kernel,
        in_specs=[full(s.shape) for s in shards],
        out_specs=[full(o.shape) for o in outs],
        out_shape=outs,
        grid=(1,),
        compiler_params=PARAMS,
        cost_estimate=CHEAP,
        name="pack",
    )(*shards)


def by_core(grads, group):
    pairs = grads.reshape(-1, 2, group, grads.shape[1])
    return pairs[:, 0], pairs[:, 1]


def natural_rows(block, group, kind):
    width = block.shape[1] // 4
    parts = [
        block[:, i * width : (i + 1) * width].astype(kind).reshape(-1, group, width)
        for i in range(4)
    ]
    return jnp.stack(parts, axis=1).reshape(-1, width).astype(LOW)


def enc_qkv_kernel(x_ref, vec_ref, w_ref, out_ref, normed):
    part = pl.program_id(0)

    @pl.when(part == 0)
    def _():
        unit, _ = norm_parts(x_ref[...].astype(F32))
        normed[...] = (unit * vec_ref[0:1, :] + vec_ref[3:4, :]).astype(LOW)

    bias = jnp.where(part == 0, vec_ref[4:5, :], jnp.where(part == 2, vec_ref[5:6, :], 0.0))
    out_ref[...] = (mm(normed[...], w_ref[...]) + bias).astype(LOW)


def enc_qkv_call(rows_in, vecs, weight):
    rows, width = rows_in.shape
    return pl.pallas_call(
        enc_qkv_kernel,
        grid=(3,),
        in_specs=[
            full((rows, width)),
            full(vecs.shape),
            pl.BlockSpec((width, width), lambda i: (0, i)),
        ],
        out_specs=pl.BlockSpec((rows, width), lambda i: (0, i)),
        out_shape=shape((rows, 3 * width), LOW),
        scratch_shapes=[pltpu.VMEM((rows, width), LOW)],
        compiler_params=PARAMS,
        cost_estimate=CHEAP,
        name="enc_qkv",
    )(rows_in, vecs, weight)


def enc_mid_kernel(
    chunks,
    packed,
    x_ref,
    att_ref,
    vec_ref,
    b1_ref,
    eb_ref,
    wo_ref,
    we_ref,
    *refs,
):
    up_ref, down_ref, *refs = refs
    mid_ref, out_ref, final_ref, act_ref, slope_ref, emb_ref, *refs = refs
    naturals, (normed, acc) = refs[:-2], refs[-2:]
    part = pl.program_id(0)

    @pl.when(part == 0)
    def _():
        middle = x_ref[...].astype(F32) + mm(att_ref[...], wo_ref[...]) + vec_ref[6:7, :]
        mid_ref[...] = middle
        unit, _ = norm_parts(middle)
        normed[...] = (unit * vec_ref[1:2, :] + vec_ref[7:8, :]).astype(LOW)
        acc[...] = middle + vec_ref[8:9, :]

    down = down_ref[...]
    if packed:
        down = natural_rows(down, packed, F32)
        naturals[0][...] = down
    hidden = mm(normed[...], up_ref[...]) + b1_ref[...]
    value, slope = gelu_parts(hidden)
    value = value.astype(LOW)
    act_ref[...] = value
    slope_ref[...] = slope
    acc[...] += mm(value, down)

    @pl.when(part == chunks - 1)
    def _():
        result = acc[...]
        out_ref[...] = result
        unit, _ = norm_parts(result)
        final = (unit * vec_ref[2:3, :] + vec_ref[9:10, :]).astype(LOW)
        final_ref[...] = final
        emb_ref[...] = (mm(final, we_ref[...]) + eb_ref[...]).astype(LOW)


def enc_mid(rows_in, attended, vecs, up_bias, emb_bias, wide, weights, proj_at, emb_at):
    rows, width = rows_in.shape
    hidden = up_bias.shape[1]
    emb_width = emb_bias.shape[1]
    chunks = hidden // width
    by_row = pl.BlockSpec((width, width), lambda i: (i, 0))
    specs = [pl.BlockSpec((width, width), lambda i: (0, i))]
    if len(weights) == 1:
        packed = width // (lax.axis_size("dp") * lax.axis_size("fsdp"))
        specs.append(pl.BlockSpec((width // 4, hidden), lambda i: (i, 1)))
        operands = [weights[0]] * 2
        natural_specs, natural_shapes = [by_row], [shape((hidden, width), LOW)]
    else:
        packed = 0
        specs.append(by_row)
        operands, natural_specs, natural_shapes = list(weights), [], []
    outs = pl.pallas_call(
        functools.partial(enc_mid_kernel, chunks, packed),
        grid=(chunks,),
        in_specs=[
            full((rows, width)),
            full((rows, width)),
            full(vecs.shape),
            pl.BlockSpec((1, width), lambda i: (0, i)),
            full((1, emb_width)),
            at_col(width, width, proj_at // width),
            at_col(width, emb_width, emb_at // emb_width),
        ]
        + specs,
        out_specs=[
            full((rows, width)),
            full((rows, width)),
            full((rows, width)),
            pl.BlockSpec((rows, width), lambda i: (0, i)),
            pl.BlockSpec((rows, width), lambda i: (0, i)),
            full((rows, emb_width)),
        ]
        + natural_specs,
        out_shape=[
            shape((rows, width), F32),
            shape((rows, width), F32),
            shape((rows, width), LOW),
            shape((rows, hidden), LOW),
            shape((rows, hidden), F32),
            shape((rows, emb_width), LOW),
        ]
        + natural_shapes,
        scratch_shapes=[pltpu.VMEM((rows, width), LOW), pltpu.VMEM((rows, width), F32)],
        compiler_params=PARAMS,
        cost_estimate=CHEAP,
        name="enc_mid",
    )(rows_in, attended, vecs, up_bias, emb_bias, wide, wide, *operands)
    return outs if packed else list(outs) + [weights[1]]


def enc_mid_back_kernel(
    chunks,
    packed,
    core_ref,
    elow_ref,
    final_ref,
    out_ref,
    mid_ref,
    att_ref,
    act_ref,
    slope_ref,
    vec_ref,
    wo_ref,
    w1_ref,
    w2_ref,
    we_ref,
    inv_ref,
    *refs,
):
    if packed:
        keep_ref, send_ref, keep2_ref, send2_ref, keep1_ref, send1_ref, *refs = refs
    else:
        keep_ref, dw2_ref, dw1_ref, *refs = refs
    (
        db1_ref,
    esum_ref,
    sum_ref,
    gmid_ref,
    gatt_ref,
    grad,
    grad_low,
    unit_two,
    scale_two,
    normed,
        dnorm,
    ) = refs
    first = core_ref[0] == 0

    def put(cols, grads):
        if packed:
            zero, one = by_core(grads, packed)
            keep_ref[:, :, cols] = jnp.where(first, zero, one).astype(LOW)
            send_ref[:, :, cols] = jnp.where(first, one, zero).astype(LOW)
        else:
            keep_ref[:, cols] = grads.astype(LOW)

    part = pl.program_id(0)

    @pl.when(part == 0)
    def _():
        elow = elow_ref[...]
        width = final_ref.shape[1]
        put(slice(width, width + elow.shape[1]), mm_tn(final_ref[...], elow))
        esum_ref[...] = jnp.zeros_like(esum_ref)
        esum_ref[0:1, :] = col_sum(elow.astype(F32))
        unit, scale = norm_parts(out_ref[...])
        dfinal = mm_nt(elow, we_ref[...])
        sum_ref[...] = jnp.zeros_like(sum_ref)
        sum_ref[0:1, :] = col_sum(dfinal * unit)
        sum_ref[1:2, :] = col_sum(dfinal)
        total = norm_back(dfinal, unit, scale, vec_ref[2:3, :])
        grad[...] = total
        low = total.astype(LOW)
        grad_low[...] = low
        sum_ref[2:3, :] = col_sum(low.astype(F32))
        unit, scale = norm_parts(mid_ref[...])
        unit_two[...] = unit
        scale_two[...] = jnp.broadcast_to(scale, scale_two.shape)
        normed[...] = (unit * vec_ref[1:2, :] + vec_ref[7:8, :]).T.astype(LOW)
        dnorm[...] = jnp.zeros_like(dnorm)

    low = grad_low[...]
    down = mm_tn(act_ref[...], low)
    if packed:
        width = low.shape[1]
        down = down.reshape(-1, 4, packed, width)
        for i in range(4):
            zero, one = by_core(down[:, i].reshape(-1, width), packed)
            cols = slice(i * width, (i + 1) * width)
            keep2_ref[:, :, cols] = jnp.where(first, zero, one).astype(LOW)
            send2_ref[:, :, cols] = jnp.where(first, one, zero).astype(LOW)
    else:
        dw2_ref[...] = down.astype(LOW)
    dhid = (slope_ref[...] * mm_nt(low, w2_ref[...])).astype(LOW)
    up = mm(normed[...], dhid)
    if packed:
        zero, one = by_core(up, packed)
        keep1_ref[...] = jnp.where(first, zero, one).astype(LOW)
        send1_ref[...] = jnp.where(first, one, zero).astype(LOW)
    else:
        dw1_ref[...] = up.astype(LOW)
    db1_ref[...] = col_sum(dhid.astype(F32))
    dnorm[...] += mm_nt(dhid, w1_ref[...])

    @pl.when(part == chunks - 1)
    def _():
        dn = dnorm[...]
        unit = unit_two[...]
        sum_ref[3:4, :] = col_sum(dn * unit)
        sum_ref[4:5, :] = col_sum(dn)
        gmid = grad[...] + norm_back(dn, unit, scale_two[:, 0:1], vec_ref[1:2, :])
        gmid_ref[...] = gmid
        mlow = gmid.astype(LOW)
        sum_ref[5:6, :] = col_sum(mlow.astype(F32))
        put(slice(0, mlow.shape[1]), mm_tn(att_ref[...], mlow))
        gatt_ref[...] = (mm_nt(mlow, wo_ref[...]) * inv_ref[...]).astype(LOW)


def enc_mid_back(
    core, elow, final, out, mid, attended, act, slope, inverse, vecs, wide, up_w, down_w, proj_at, emb_at
):
    rows, width = mid.shape
    hidden = down_w.shape[0]
    emb_width = elow.shape[1]
    chunks = hidden // width
    packed = width // (lax.axis_size("dp") * lax.axis_size("fsdp"))
    packed = packed if packed % 8 == 0 else 0
    by_col = pl.BlockSpec((rows, width), lambda i: (0, i))
    if packed:
        chips = width // packed // 2
        two = pl.BlockSpec((chips // chunks, packed, hidden), lambda i: (i, 0, 0))
        one = pl.BlockSpec((chips, packed, width), lambda i: (0, 0, i))
        side = (chips, packed, width + emb_width)
        specs = [full(side), full(side), two, two, one, one]
        shapes = [shape(side, LOW)] * 2 + [shape((chips, packed, hidden), LOW)] * 4
    else:
        specs = [
            full((width, width + emb_width)),
            pl.BlockSpec((width, width), lambda i: (i, 0)),
            pl.BlockSpec((width, width), lambda i: (0, i)),
        ]
        shapes = [
            shape((width, width + emb_width), LOW),
            shape((hidden, width), LOW),
            shape((width, hidden), LOW),
        ]
    return pl.pallas_call(
        functools.partial(enc_mid_back_kernel, chunks, packed),
        grid=(chunks,),
        in_specs=[
            pl.BlockSpec(memory_space=pltpu.SMEM),
            full((rows, emb_width)),
            full((rows, width)),
            full((rows, width)),
            full((rows, width)),
            full((rows, width)),
            by_col,
            by_col,
            full(vecs.shape),
            at_col(width, width, proj_at // width),
            pl.BlockSpec((width, width), lambda i: (0, i)),
            pl.BlockSpec((width, width), lambda i: (i, 0)),
            at_col(width, emb_width, emb_at // emb_width),
            full((rows, width)),
        ],
        out_specs=[
            *specs,
            pl.BlockSpec((1, width), lambda i: (0, i)),
            full((8, emb_width)),
            full((8, width)),
            full((rows, width)),
            full((rows, width)),
        ],
        out_shape=[
            *shapes,
            shape((1, hidden), F32),
            shape((8, emb_width), F32),
            shape((8, width), F32),
            shape((rows, width), F32),
            shape((rows, width), LOW),
        ],
        scratch_shapes=[
            pltpu.VMEM((rows, width), F32),
            pltpu.VMEM((rows, width), LOW),
            pltpu.VMEM((rows, width), F32),
            pltpu.VMEM((rows, LANES), F32),
            pltpu.VMEM((width, rows), LOW),
            pltpu.VMEM((rows, width), F32),
        ],
        compiler_params=PARAMS,
        cost_estimate=CHEAP,
        name="enc_mid_back",
    )(core, elow, final, out, mid, attended, act, slope, vecs, wide, up_w, down_w, wide, inverse)


def enc_qkv_back_kernel(
    packed,
    core_ref,
    x_ref,
    dq_ref,
    dk_ref,
    dv_ref,
    gmid_ref,
    vec_ref,
    more_ref,
    w_ref,
    din_ref,
    *refs,
):
    outs, sums = refs[:-1], refs[-1]
    first = core_ref[0] == 0
    width = x_ref.shape[1]

    cut = outs[0].shape[-1]

    def put(ref, cols, grads):
        if packed:
            zero, one = by_core(grads, packed)
            outs[ref][:, :, cols] = jnp.where(first, zero, one).astype(LOW)
            outs[ref + 2][:, :, cols] = jnp.where(first, one, zero).astype(LOW)
        else:
            outs[ref][:, cols] = grads.astype(LOW)

    unit, scale = norm_parts(x_ref[...].astype(F32))
    normed = (unit * vec_ref[0:1, :] + vec_ref[3:4, :]).astype(LOW)
    grads = jnp.concatenate([dq_ref[...], dk_ref[...], dv_ref[...]], axis=1)
    weight_grad = mm_tn(normed, grads)
    put(0, slice(0, cut), weight_grad[:, :cut])
    put(1, slice(0, 3 * width - cut), weight_grad[:, cut:])
    dn = mm_nt(grads, w_ref[...])
    sums[...] = jnp.zeros_like(sums)
    sums[0:16, :] = more_ref[...]
    sums[0:1, :] = col_sum(dn * unit)
    sums[3:4, :] = col_sum(dn)
    sums[4:5, :] = col_sum(dq_ref[...].astype(F32))
    sums[5:6, :] = col_sum(dv_ref[...].astype(F32))
    put(1, slice(3 * width - cut, 3 * width - cut + LANES), sums[...].T)
    din = gmid_ref[...] + norm_back(dn, unit, scale, vec_ref[0:1, :])
    din_ref[...] = din.astype(LOW)


def enc_qkv_back(core, rows_in, dq, dk, dv, gmid, vecs, more, weight):
    rows, width = rows_in.shape
    whole = full((rows, width))
    cut = (3 * width + LANES) // 2 // LANES * LANES
    halves = [cut, 3 * width + LANES - cut]
    packed = width // (lax.axis_size("dp") * lax.axis_size("fsdp"))
    packed = packed if packed % 8 == 0 else 0
    if packed:
        outs = [(width // packed // 2, packed, cols) for cols in halves * 2]
    else:
        outs = [(width, cols) for cols in halves]
    return pl.pallas_call(
        functools.partial(enc_qkv_back_kernel, packed),
        grid=(1,),
        in_specs=[pl.BlockSpec(memory_space=pltpu.SMEM)]
        + [whole] * 5
        + [full(vecs.shape), full((16, width)), at_col(width, 3 * width, 0)],
        out_specs=[whole] + [full(o) for o in outs],
        out_shape=[shape((rows, width), LOW)] + [shape(o, LOW) for o in outs],
        scratch_shapes=[pltpu.VMEM((LANES, width), F32)],
        compiler_params=PARAMS,
        cost_estimate=CHEAP,
        name="enc_qkv_back",
    )(core, rows_in, dq, dk, dv, gmid, vecs, more, weight)


def dec_in_kernel(
    limit,
    each,
    order_ref,
    line_ref,
    core_ref,
    own_one,
    own_two,
    got_one,
    got_two,
    pos_ref,
    vec_ref,
    w_ref,
    in_ref,
    qkv_ref,
):
    step = pl.program_id(0)
    width = in_ref.shape[1]
    for half, (own, got) in enumerate(((own_one, got_one), (own_two, got_two))):
        place = order_ref[0, 2 * step + half]
        rows = slice(half * BLOCK, (half + 1) * BLOCK)
        block = jnp.where(place // each % 2 == core_ref[0], own[0], got[0]).astype(F32)
        in_ref[rows, :] = jnp.where(place < limit, block, vec_ref[9:10, :]) + pos_ref[rows, :]
    unit, _ = norm_parts(in_ref[...])
    normed = (unit * vec_ref[0:1, :] + vec_ref[3:4, :]).astype(LOW)
    qkv = mm(normed, w_ref[...])
    qkv_ref[:, :width] = (qkv[:, :width] + vec_ref[4:5, :]).astype(LOW)
    qkv_ref[:, width : 2 * width] = qkv[:, width : 2 * width].astype(LOW)
    qkv_ref[:, 2 * width :] = (qkv[:, 2 * width :] + vec_ref[5:6, :]).astype(LOW)


def dec_in_call(order, line, core, own, got, pos, vecs, weight):
    rows, width = pos.shape
    each = own.shape[1] // BLOCK
    limit = 2 * own.shape[0] * each

    def chosen(half):
        def index(i, order_ref, line_ref):
            place = jnp.clip(order_ref[0, 2 * i + half], 0, limit - 1)
            chip = lax.rem(line_ref[0] - place // each // 2 + own.shape[0], own.shape[0])
            return (chip, place % each, 0)

        return pl.BlockSpec((1, BLOCK, width), index)

    return pl.pallas_call(
        functools.partial(dec_in_kernel, limit, each),
        grid_spec=pltpu.PrefetchScalarGridSpec(
            num_scalar_prefetch=2,
            grid=(rows // TILE,),
            in_specs=[
                pl.BlockSpec(memory_space=pltpu.SMEM),
                chosen(0),
                chosen(1),
                chosen(0),
                chosen(1),
                pl.BlockSpec((TILE, width), lambda i, o, z: (i, 0)),
                full(vecs.shape),
                at_col(width, 3 * width, 0),
            ],
            out_specs=[
                pl.BlockSpec((TILE, width), lambda i, o, z: (i, 0)),
                pl.BlockSpec((TILE, 3 * width), lambda i, o, z: (i, 0)),
            ],
        ),
        out_shape=[shape((rows, width), F32), shape((rows, 3 * width), LOW)],
        compiler_params=PARAMS,
        cost_estimate=CHEAP,
        name="dec_in",
    )(order, line, core, own, own, got, got, pos, vecs, weight)


def dec_mid_kernel(
    steps,
    chunks,
    packed,
    x_ref,
    att_ref,
    cot_ref,
    inv_ref,
    vec_ref,
    b1_ref,
    wo_ref,
    up_ref,
    down_ref,
    out_ref,
    gmid_ref,
    gatt_ref,
    dw_ref,
    db1_ref,
    sum_ref,
    aw1,
    aw2,
    acc,
    dnorm,
    turned,
):
    step = pl.program_id(0)
    width = x_ref.shape[1]
    hidden = chunks * width
    lead = width // 4

    @pl.when(step == 0)
    def _():
        aw1[...] = jnp.zeros_like(aw1)
        aw2[...] = jnp.zeros_like(aw2)
        db1_ref[...] = jnp.zeros_like(db1_ref)
        sum_ref[...] = jnp.zeros_like(sum_ref)

    att = att_ref[...]
    low = cot_ref[...]
    middle = x_ref[...] + mm(att, wo_ref[...]) + vec_ref[6:7, :]
    unit, scale = norm_parts(middle)
    normed = unit * vec_ref[1:2, :] + vec_ref[7:8, :]
    turned[...] = normed.T.astype(LOW)
    normed = normed.astype(LOW)
    acc[...] = middle + vec_ref[8:9, :]
    dnorm[...] = jnp.zeros_like(dnorm)

    def chunk(j, carry):
        cols = pl.ds(pl.multiple_of(j * width, width), width)
        some = pl.ds(pl.multiple_of(j * lead, lead), lead)
        up = up_ref[:, cols]
        down = natural_rows(down_ref[some, :], packed, LOW) if packed else down_ref[cols, :]
        value, slope = gelu_parts(mm(normed, up) + b1_ref[j])
        value = value.astype(LOW)
        acc[...] += mm(value, down)
        grad = mm_tn(value, low)
        if packed:
            grad = grad.reshape(-1, 4, packed, width)
            for part in range(4):
                piece = grad[:, part].reshape(lead, width)
                aw2[some, part * width : (part + 1) * width] += piece
        else:
            aw2[cols, :] += grad
        dhid = (slope * mm_nt(low, down)).astype(LOW)
        aw1[:, cols] += mm(turned[...], dhid)
        db1_ref[j] += col_sum(dhid.astype(F32))
        dnorm[...] += mm_nt(dhid, up)
        return carry

    lax.fori_loop(0, chunks, chunk, 0, unroll=2)
    out_ref[...] = acc[...].astype(LOW)
    dn = dnorm[...]
    sum_ref[0:1, :] += col_sum(dn * unit)
    sum_ref[1:2, :] += col_sum(dn)
    gmid = low.astype(F32) + norm_back(dn, unit, scale, vec_ref[1:2, :])
    gmid_ref[...] = gmid
    mlow = gmid.astype(LOW)
    sum_ref[2:3, :] += col_sum(mlow.astype(F32))
    sum_ref[3:4, :] += col_sum(low.astype(F32))
    aw1[:, hidden:] += mm_tn(att, mlow)
    gatt_ref[...] = (mm_nt(mlow, wo_ref[...]) * inv_ref[...]).astype(LOW)

    @pl.when(step == steps - 1)
    def _():
        dw_ref[:, : hidden + width] = aw1[...].astype(LOW)
        if packed:
            dw_ref[:, hidden + width :] = aw2[...].astype(LOW)
        else:
            for c in range(chunks):
                col = hidden + (1 + c) * width
                dw_ref[:, col : col + width] = aw2[c * width : (c + 1) * width, :].astype(LOW)


def dec_mid(dec_in, attended, cotangent, inverse, vecs, up_bias, wide, weights, proj_at):
    rows, width = dec_in.shape
    hidden = up_bias.shape[1]
    chunks = hidden // width
    tile = 2 * TILE
    steps = rows // tile
    by_row = pl.BlockSpec((tile, width), lambda i: (i, 0))
    if len(weights) == 1:
        packed = width // (lax.axis_size("dp") * lax.axis_size("fsdp"))
        down_shape = (width, hidden)
        specs, operands = [at_col(width, hidden, 0), at_col(width, hidden, 1)], [weights[0]] * 2
    else:
        packed, down_shape = 0, (hidden, width)
        specs, operands = [full((width, hidden)), full(down_shape)], list(weights)
    return pl.pallas_call(
        functools.partial(dec_mid_kernel, steps, chunks, packed),
        grid=(steps,),
        in_specs=[
            by_row,
            by_row,
            by_row,
            by_row,
            full(vecs.shape),
            full((chunks, 1, width)),
            at_col(width, width, proj_at // width),
        ]
        + specs,
        out_specs=[
            by_row,
            by_row,
            by_row,
            full((width, 2 * hidden + width)),
            full((chunks, 1, width)),
            full((8, width)),
        ],
        out_shape=[
            shape((rows, width), LOW),
            shape((rows, width), F32),
            shape((rows, width), LOW),
            shape((width, 2 * hidden + width), LOW),
            shape((chunks, 1, width), F32),
            shape((8, width), F32),
        ],
        scratch_shapes=[
            pltpu.VMEM((width, hidden + width), F32),
            pltpu.VMEM(down_shape, F32),
            pltpu.VMEM((tile, width), F32),
            pltpu.VMEM((tile, width), F32),
            pltpu.VMEM((width, tile), LOW),
        ],
        compiler_params=PARAMS,
        cost_estimate=CHEAP,
        name="dec_mid",
    )(
        dec_in,
        attended,
        cotangent,
        inverse,
        vecs,
        up_bias.reshape(chunks, 1, width),
        wide,
        *operands,
    )


def dec_back_kernel(
    limit,
    each,
    order_ref,
    core_ref,
    x_ref,
    dq_ref,
    dk_ref,
    dv_ref,
    gmid_ref,
    vec_ref,
    more_ref,
    w_ref,
    sum_ref,
    keep_ref,
    send_ref,
):
    step = pl.program_id(0)

    @pl.when(step == 0)
    def _():
        sum_ref[...] = more_ref[...]
        keep_ref[...] = jnp.zeros_like(keep_ref)
        send_ref[...] = jnp.zeros_like(send_ref)

    unit, scale = norm_parts(x_ref[...])
    grads = jnp.concatenate([dq_ref[...], dk_ref[...], dv_ref[...]], axis=1)
    dn = mm_nt(grads, w_ref[...])
    sum_ref[0:1, :] += col_sum(dn * unit)
    sum_ref[2:3, :] += col_sum(dn)
    sum_ref[3:4, :] += col_sum(dq_ref[...].astype(F32))
    sum_ref[4:5, :] += col_sum(dv_ref[...].astype(F32))
    din = gmid_ref[...] + norm_back(dn, unit, scale, vec_ref[0:1, :])
    per = x_ref.shape[0] // BLOCK
    for b in range(per):
        place = order_ref[0, per * step + b]
        rows = din[b * BLOCK : (b + 1) * BLOCK, :]

        owner = place // each
        spot = pl.ds(pl.multiple_of(place % each * BLOCK, BLOCK), BLOCK)

        @pl.when((place < limit) & (owner % 2 == core_ref[0]))
        def _():
            keep_ref[owner // 2, spot, :] = rows.astype(LOW)

        @pl.when((place < limit) & (owner % 2 != core_ref[0]))
        def _():
            send_ref[owner // 2, spot, :] = rows.astype(LOW)

        @pl.when(place >= limit)
        def _():
            sum_ref[8:9, :] += col_sum(rows)


def dec_back(order, core, dec_in, dq, dk, dv, gmid, vecs, more, weight, limit, each):
    rows, width = dec_in.shape
    tile = TILE
    by_row = pl.BlockSpec((tile, width), lambda i, o: (i, 0))
    side = (limit // each // 2, each * BLOCK, width)
    return pl.pallas_call(
        functools.partial(dec_back_kernel, limit, each),
        grid_spec=pltpu.PrefetchScalarGridSpec(
            num_scalar_prefetch=1,
            grid=(rows // tile,),
            in_specs=[pl.BlockSpec(memory_space=pltpu.SMEM)]
            + [by_row] * 5
            + [full(vecs.shape), full((16, width)), at_col(width, 3 * width, 0)],
            out_specs=[full((16, width)), full(side), full(side)],
        ),
        out_shape=[shape((16, width), F32), shape(side, LOW), shape(side, LOW)],
        compiler_params=PARAMS,
        cost_estimate=CHEAP,
        name="dec_back",
    )(order, core, dec_in, dq, dk, dv, gmid, vecs, more, weight)


def dec_grad_kernel(x_ref, dq_ref, dk_ref, dv_ref, vec_ref, sum_ref, dw_ref, acc, sums):
    step = pl.program_id(0)
    width = x_ref.shape[1]

    @pl.when(step == 0)
    def _():
        acc[...] = jnp.zeros_like(acc)

    unit, _ = norm_parts(x_ref[...])
    normed = (unit * vec_ref[0:1, :] + vec_ref[3:4, :]).astype(LOW)
    grads = jnp.concatenate([dq_ref[...], dk_ref[...], dv_ref[...]], axis=1)
    acc[...] += mm_tn(normed, grads)

    @pl.when(step == pl.num_programs(0) - 1)
    def _():
        dw_ref[:, : 3 * width] = acc[...].astype(LOW)
        sums[...] = jnp.zeros_like(sums)
        sums[0:16, :] = sum_ref[...]
        dw_ref[:, 3 * width :] = sums[...].T.astype(LOW)


def dec_grad(dec_in, dq, dk, dv, vecs, sums):
    rows, width = dec_in.shape
    tile = 2 * TILE
    by_row = pl.BlockSpec((tile, width), lambda i: (i, 0))
    packed = (width, 3 * width + LANES)
    return pl.pallas_call(
        dec_grad_kernel,
        grid=(rows // tile,),
        in_specs=[by_row] * 4 + [full(vecs.shape), full((16, width))],
        out_specs=full(packed),
        out_shape=shape(packed, LOW),
        scratch_shapes=[pltpu.VMEM((width, 3 * width), F32), pltpu.VMEM((LANES, width), F32)],
        compiler_params=PARAMS,
        cost_estimate=CHEAP,
        name="dec_grad",
    )(dec_in, dq, dk, dv, vecs, sums)


def positions(count, width):
    places = jnp.arange(count, dtype=jnp.float32)[:, None]
    columns = jnp.arange(width)
    rates = jnp.exp((2 * (columns // 2)).astype(jnp.float32) * (-math.log(10000.0) / width))
    angles = places * rates[None, :]
    return jnp.where((columns % 2 == 0)[None, :], jnp.sin(angles), jnp.cos(angles))


def bits_of(axis):
    size, out = lax.axis_size(axis), []
    while size > 1:
        size //= 2
        out.append((axis, size))
    return out


def all_bits():
    return bits_of("dp") + bits_of("fsdp")


def bit_here(bit):
    axis, stride = bit
    return lax.axis_index(axis) // stride % 2


def swap(value, bit):
    axis, stride = bit
    return lax.ppermute(value, axis, [(i, i ^ stride) for i in range(lax.axis_size(axis))])


def pair(own, got, here, dim):
    dims = tuple(2 if d == dim else 1 for d in range(own.ndim + 1))
    mine = lax.broadcasted_iota(jnp.int32, dims, dim) == here
    return jnp.where(mine, jnp.expand_dims(own, dim), jnp.expand_dims(got, dim))


class Gather:
    def __init__(self, piece, order, held=()):
        self.piece, self.order, self.held = piece, list(order), list(held)

    def begin(self):
        self.got = swap(self.piece, self.order[0])

    def finish(self):
        canon, bit = all_bits(), self.order.pop(0)
        dim = sum(canon.index(b) < canon.index(bit) for b in self.held)
        self.piece = pair(self.piece, self.got, bit_here(bit), dim)
        self.held.append(bit)

    def step(self):
        self.begin()
        self.finish()

    def end_beside(self, outputs):
        self.got, outputs = lax.optimization_barrier((self.got, outputs))
        self.finish()
        return outputs

    def rest(self):
        while self.order:
            self.step()
        return self.piece

    def tie(self, other):
        self.piece, other = lax.optimization_barrier((self.piece, other))
        return other


def gather(piece, order, held=()):
    return Gather(piece, order, held).rest()


def along_line(value, by):
    size = lax.axis_size("fsdp")
    return lax.ppermute(value, "fsdp", [(i, (i + 2 * by) % size) for i in range(size)])


def join(pieces, bit):
    both = [pair(own, swap(own, bit), bit_here(bit), own.ndim - 2) for own in pieces]
    both = both[0] if len(both) == 1 else jnp.concatenate(both, axis=-1)
    return both.reshape(-1, both.shape[-1])


def term_sum(terms, kind):
    total = terms[0].astype(F32)
    for term in terms[1:]:
        total = total + term.astype(F32)
    return total.astype(kind)


class Fold:
    def __init__(self, terms, order, held=None):
        self.terms, self.order, self.send = list(terms), list(order), None
        self.left = list(all_bits() if held is None else held)

    def cut(self):
        if self.send is not None:
            return
        bit = self.order[0]
        dim = self.left.index(bit)
        here = bit_here(bit)

        def half(index):
            return [lax.dynamic_index_in_dim(t, index, dim, keepdims=False) for t in self.terms]

        self.send, self.terms = term_sum(half(1 - here), LOW), half(here)

    def pass_on(self):
        bit = self.order.pop(0)
        self.left.remove(bit)
        self.terms.append(swap(self.send, bit))
        self.send = None


def split_fold(keep, send, order, held=None):
    held = all_bits() if held is None else held
    dims = (2,) * (len(held) - 1) + keep.shape[-2:]
    fold = Fold([keep.reshape(dims)], order, held)
    fold.send = send.reshape(dims)
    return fold


def start_beside(folds, inputs):
    for fold in folds:
        fold.cut()
    sends, inputs = lax.optimization_barrier(([f.send for f in folds], inputs))
    for fold, send in zip(folds, sends):
        fold.send = send
        fold.pass_on()
    return inputs


def end_beside(folds, outputs):
    last, outputs = lax.optimization_barrier(([f.terms[-1] for f in folds], outputs))
    for fold, got in zip(folds, last):
        fold.terms[-1] = got
    return outputs


def one_round(folds):
    for fold in folds:
        fold.cut()
        fold.pass_on()
    end_beside(folds, ())


def joined(folds, line):
    terms = [term_sum(f.terms, F32) for f in folds]
    return Fold([jnp.concatenate(terms, axis=-1)], line[::-1], line)


def by_bits(grads):
    bits = len(all_bits())
    rows = grads.shape[0] >> bits
    return grads.reshape((2,) * bits + (rows, grads.shape[1]))


def pack_vectors(pieces, rows):
    wide = jnp.concatenate([p.reshape(-1, rows) for p in pieces], axis=0)
    wide = jnp.pad(wide, ((0, LANES - wide.shape[0]), (0, 0)))
    return wide.T


def unpack_tall(columns, devices, width):
    rows = columns.shape[0] // devices
    parts = columns.shape[1] // width
    return (
        columns.reshape(devices, rows, parts, width)
        .transpose(0, 2, 1, 3)
        .reshape(devices * parts * rows, width)
    )


def repack_tall(weight, devices, rows):
    parts = weight.shape[0] // (devices * rows)
    width = weight.shape[1]
    return (
        weight.reshape(devices, parts, rows, width)
        .transpose(0, 2, 1, 3)
        .reshape(devices * rows, parts * width)
    )


def split_columns(array, widths):
    out, at = [], 0
    for w in widths:
        out.append(array[:, at : at + w])
        at += w
    return out


def long_vector(rows_of, devices):
    parts, total = rows_of.shape
    return rows_of.reshape(parts, devices, total // devices).transpose(1, 0, 2).reshape(1, -1)


def long_rows(vector, devices, rows):
    parts = vector.shape[0] // (devices * rows)
    return vector.reshape(devices, parts, rows).transpose(1, 0, 2).reshape(parts, -1)


def per_device(
    enc_input,
    enc_segments,
    dec_segments,
    block_order,
    dec_cotangent,
    enc_qkv,
    enc_proj,
    enc_fc1,
    enc_fc2,
    enc_gains,
    enc_biases,
    enc_fc1_bias,
    embed,
    mask_token,
    dec_qkv,
    dec_proj,
    dec_fc1,
    dec_fc2,
    dec_gains,
    dec_biases,
    dec_fc1_bias,
    dec_fc2_bias,
):
    devices = lax.axis_size("dp") * lax.axis_size("fsdp")
    enc_rows, width = enc_input.shape
    dec_rows, dwidth = dec_cotangent.shape
    erows = enc_qkv.shape[0]
    drows = dec_qkv.shape[0]
    ff = enc_fc1.shape[1]
    dff = dec_fc1.shape[1]
    emb_row = jnp.pad(dec_biases[0], (0, erows - drows))
    enc_first = jnp.concatenate(
        [
            enc_qkv,
            enc_proj,
            embed,
            pack_vectors([enc_gains, enc_biases, enc_fc1_bias, emb_row], erows),
        ],
        axis=1,
    )
    dec_first = jnp.concatenate(
        [
            dec_qkv,
            dec_proj,
            pack_vectors(
                [dec_gains, dec_biases, dec_fc2_bias[None], mask_token[None], dec_fc1_bias], drows
            ),
        ],
        axis=1,
    )
    proj_at, emb_at = 3 * width, 4 * width
    vec_at = emb_at + dwidth
    dproj_at, dvec_at = 3 * dwidth, 4 * dwidth
    ecut = (vec_at + LANES) // 2 // LANES * LANES
    here = bit_here(bits_of("fsdp")[-1]).reshape(1)
    chips = lax.axis_size("fsdp") // 2
    chip = lax.axis_index("fsdp") // 2
    dp, fsdp = bits_of("dp"), bits_of("fsdp")
    line, core = fsdp[:-1], fsdp[-1]
    packed = erows % 8 == 0 and drows % 16 == 0
    enc_rest, dec_rest = [enc_fc1, enc_fc2], [dec_fc1, dec_fc2]
    if packed:
        enc_rest, dec_rest = ([w] for w in pack_shards(*enc_rest, *dec_rest))
    enc_rest = [lax.all_gather(w, AXES, axis=0, tiled=True) for w in enc_rest]
    lined = gather(enc_first, line)
    one = Gather(lined[..., :ecut], dp[::-1], line)
    two = Gather(lined[..., ecut:], dp, line)
    one.begin()
    two.begin()
    pos = positions(dec_rows, dwidth)
    pos = one.end_beside(pos)
    two.finish()
    while one.order:
        one.step()
        two.step()
    dec_gather = Gather(dec_first, line + dp)
    one.piece = dec_gather.tie(one.piece)
    dec_gather.begin()
    enc_all = join([one.piece, two.piece], core)
    enc_all = dec_gather.end_beside(enc_all)
    while len(dec_gather.order) > 3:
        dec_gather.step()
    evecs = enc_all[:, vec_at:].T[:16].astype(F32)
    up_bias = long_vector(evecs[10:14], devices)
    emb_bias = evecs[14].reshape(devices, erows)[:, :drows].reshape(1, -1)

    enc_all, evecs = dec_gather.tie((enc_all, evecs))
    dec_gather.begin()
    qkv = enc_qkv_call(enc_input, evecs, enc_all)
    enc_col = enc_segments.reshape(-1, 1)
    qkv = dec_gather.end_beside(qkv)
    dec_gather.begin()
    attended, inverse, weights = attend(qkv, enc_segments, enc_col, HDIM)
    attended = dec_gather.end_beside(attended)
    dec_gather.begin()
    mid, enc_out, final, act, slope, embedded, down_w = enc_mid(
        enc_input,
        attended,
        evecs,
        up_bias,
        emb_bias,
        enc_all,
        enc_rest,
        proj_at,
        emb_at,
    )
    embedded, dec_rest = dec_gather.end_beside((embedded, dec_rest))
    emb_got = [along_line(embedded, by) for by in range(1, chips)]
    dec_rest = [lax.all_gather(w, AXES, axis=0, tiled=True) for w in dec_rest]
    dec_got = swap(dec_gather.piece, core)
    dim = dec_got.ndim - 2
    dec_all = pair(dec_gather.piece, dec_got, bit_here(core), dim)
    dec_all = dec_all.reshape(-1, dec_got.shape[-1])
    dvecs = pair(dec_gather.piece[..., dvec_at:], dec_got[..., dvec_at:], bit_here(core), dim)
    dvecs = dvecs.reshape(-1, LANES).T[:16].astype(F32)
    dup_bias = long_vector(dvecs[10:14], devices)
    emb_got, dec_all, dvecs, dup_bias = lax.optimization_barrier(
        (emb_got, dec_all, dvecs, dup_bias)
    )
    emb_own = jnp.stack([embedded] + emb_got)
    emb_got = swap(emb_own, core)
    limit = 2 * chips * enc_rows // BLOCK
    dec_in, dqkv = dec_in_call(
        block_order, chip.reshape(1), here, emb_own, emb_got, pos, dvecs, dec_all
    )
    dec_col = dec_segments.reshape(-1, 1)
    dattended, dinverse, dweights = attend(dqkv, dec_segments, dec_col, DHDIM)
    dec_out, dgmid, dgatt, dw_rest, db1, dsum_mid = dec_mid(
        dec_in,
        dattended,
        dec_cotangent,
        dinverse,
        dvecs,
        dup_bias,
        dec_all,
        dec_rest,
        dproj_at,
    )
    if not packed:
        chunks = dff // dwidth
        tall = dw_rest[:, dff + dwidth :].reshape(dwidth, chunks, dwidth).transpose(1, 0, 2)
        tall = repack_tall(tall.reshape(dff, dwidth), devices, drows)
        dw_rest = jnp.concatenate([dw_rest[:, : dff + dwidth], tall], axis=1)
    dec_own = lax.psum_scatter(dw_rest, "dp", scatter_dimension=0, tiled=True)
    dec_more = jnp.concatenate(
        [
            jnp.zeros((1, dwidth), F32),
            dsum_mid[0:1],
            jnp.zeros((3, dwidth), F32),
            dsum_mid[2:3],
            dsum_mid[1:2],
            dsum_mid[3:4],
            jnp.zeros((1, dwidth), F32),
            long_rows(db1.reshape(-1), devices, drows),
            jnp.zeros((3, dwidth), F32),
        ],
        axis=0,
    )
    dgatt, dec_more = lax.optimization_barrier((dgatt, dec_more))
    ddq, ddk, ddv = attend_back(dqkv, dattended, dgatt, dweights, dec_segments, DHDIM)
    dsum, keep, send = dec_back(
        block_order,
        here,
        dec_in,
        ddq,
        ddk,
        ddv,
        dgmid,
        dvecs,
        dec_more,
        dec_all,
        limit,
        enc_rows // BLOCK,
    )
    emb_terms, dsum = lax.optimization_barrier((swap(send, core), dsum))
    emb_terms = [keep, emb_terms]

    def piece_of(place):
        return [lax.dynamic_index_in_dim(t, place % chips, 0, keepdims=False) for t in emb_terms]

    emb_back = [along_line(term_sum(piece_of(chip + by), LOW), by) for by in range(1, chips)]
    dec_grads = dec_grad(dec_in, ddq, ddk, ddv, dvecs, dsum)
    emb_back, dec_grads, dec_own = lax.optimization_barrier((emb_back, dec_grads, dec_own))
    dec_grads = lax.psum_scatter(dec_grads, "dp", scatter_dimension=0, tiled=True)
    elow = term_sum(piece_of(chip) + emb_back, LOW)
    *ew, eb1, esum_emb, esum_mid, gmid, gatt = enc_mid_back(
        here,
        elow,
        final,
        enc_out,
        mid,
        attended,
        act,
        slope,
        inverse,
        evecs,
        enc_all,
        enc_rest[0],
        down_w,
        proj_at,
        emb_at,
    )
    gatt, dec_own, dec_grads = lax.optimization_barrier((gatt, dec_own, dec_grads))
    dec_own = jnp.concatenate([dec_own, dec_grads], axis=1)
    dec_own = lax.psum_scatter(dec_own, "fsdp", scatter_dimension=0, tiled=True)
    spread = [core] + line[::-1] + dp
    if packed:
        early = split_fold(ew[0], ew[1], spread)
        edown = split_fold(ew[2], ew[3], [core] + dp[::-1])
        eup = split_fold(ew[4], ew[5], [core] + dp)
    else:
        early = Fold([by_bits(ew[0])], spread)
        edown = Fold([by_bits(repack_tall(ew[1], devices, erows))], [core] + dp[::-1])
        eup = Fold([by_bits(ew[2])], [core] + dp)
    side = [eup, edown, early]
    for fold in side:
        fold.cut()
        fold.pass_on()
    emb_sum = jnp.pad(esum_emb[0].reshape(devices, drows), ((0, 0), (0, erows - drows)))
    enc_more = jnp.concatenate(
        [
            jnp.zeros((1, width), F32),
            esum_mid[3:4],
            esum_mid[0:1],
            jnp.zeros((3, width), F32),
            esum_mid[5:6],
            esum_mid[4:5],
            esum_mid[2:3],
            esum_mid[1:2],
            long_rows(eb1.reshape(-1), devices, erows),
            emb_sum.reshape(1, -1),
            jnp.zeros((1, width), F32),
        ],
        axis=0,
    )
    gatt, enc_more = end_beside(side, (gatt, enc_more))
    gatt, early.terms[-1] = start_beside([eup, edown], (gatt, early.terms[-1]))
    gatt = start_beside([early], gatt)
    dq, dk, dv = attend_back(qkv, attended, gatt, weights, enc_segments, HDIM)
    enc_in_grad, *enc_grads = enc_qkv_back(
        here, enc_input, dq, dk, dv, gmid, evecs, enc_more, enc_all
    )
    if packed:
        halves = [split_fold(enc_grads[i], enc_grads[i + 2], [core]) for i in range(2)]
    else:
        halves = [Fold([by_bits(grads)], [core]) for grads in enc_grads]
        for half in halves:
            half.cut()
    sends, dec_own = end_beside(side, ([half.send for half in halves], dec_own))
    for half, half.send in zip(halves, sends):
        half.pass_on()
    while eup.order:
        one_round(side)
    end_beside(halves, ())
    one = Fold(halves[0].terms, dp, all_bits()[:-1])
    two = Fold(halves[1].terms, dp[::-1], all_bits()[:-1])
    for fold in (one, two):
        fold.cut()
    sends, last = lax.optimization_barrier(
        ([one.send, two.send], [eup.terms[-1], edown.terms[-1]])
    )
    one.send, two.send = sends
    eup.terms[-1], edown.terms[-1] = last
    rest = joined([eup, edown], line)
    one_round([one, two, rest, early])
    if rest.order:
        rest.cut()
        rest.pass_on()
    while one.order or early.order:
        one_round([f for f in (one, two, early) if f.order])
    first = joined([one, two], line)
    first.cut()
    first.pass_on()
    end_beside([first, rest], ())
    while first.order or rest.order:
        one_round([f for f in (first, rest) if f.order])
    ep, em = split_columns(term_sum(early.terms, F32), [width, dwidth])
    eu, ed = split_columns(term_sum(rest.terms, F32), [ff, ff])
    ed = unpack_tall(ed, 1, width)
    eq, ev = split_columns(term_sum(first.terms, F32), [3 * width, LANES])
    ru, rp, rd, rq, rv = split_columns(
        dec_own.astype(F32), [dff, dwidth, dff, 3 * dwidth, LANES]
    )
    rd = unpack_tall(rd, 1, dwidth)
    rv = rv.T
    ev = ev.T
    return (
        dec_out,
        enc_in_grad,
        eq,
        ep,
        eu,
        ed,
        ev[:3],
        ev[3:10],
        ev[10:14].reshape(-1),
        em,
        rv[8],
        rq,
        rp,
        ru,
        rd,
        rv[:2],
        jnp.concatenate([ev[14:15, :drows], rv[2:7]], axis=0),
        rv[9:13].reshape(-1),
        rv[7],
    )


def solution(mesh):
    in_specs = (
        P(("dp", "fsdp"), None),
        P(("dp", "fsdp"), None),
        P(("dp", "fsdp"), None),
        P("dp", "fsdp"),
        P(("dp", "fsdp"), None),
        P(("dp", "fsdp"), None),
        P(("dp", "fsdp"), None),
        P(("dp", "fsdp"), None),
        P(("dp", "fsdp"), None),
        P(None, ("dp", "fsdp")),
        P(None, ("dp", "fsdp")),
        P(("dp", "fsdp")),
        P(("dp", "fsdp"), None),
        P(("dp", "fsdp")),
        P(("dp", "fsdp"), None),
        P(("dp", "fsdp"), None),
        P(("dp", "fsdp"), None),
        P(("dp", "fsdp"), None),
        P(None, ("dp", "fsdp")),
        P(None, ("dp", "fsdp")),
        P(("dp", "fsdp")),
        P(("dp", "fsdp")),
    )
    out_specs = (
        P(("dp", "fsdp"), None),
        P(("dp", "fsdp"), None),
        P(("dp", "fsdp"), None),
        P(("dp", "fsdp"), None),
        P(("dp", "fsdp"), None),
        P(("dp", "fsdp"), None),
        P(None, ("dp", "fsdp")),
        P(None, ("dp", "fsdp")),
        P(("dp", "fsdp")),
        P(("dp", "fsdp"), None),
        P(("dp", "fsdp")),
        P(("dp", "fsdp"), None),
        P(("dp", "fsdp"), None),
        P(("dp", "fsdp"), None),
        P(("dp", "fsdp"), None),
        P(None, ("dp", "fsdp")),
        P(None, ("dp", "fsdp")),
        P(("dp", "fsdp")),
        P(("dp", "fsdp")),
    )
    return jax.shard_map(
        per_device, mesh=mesh, in_specs=in_specs, out_specs=out_specs, check_vma=False
    )
```

profile of v0, /device:TPU:0, one launch (start us, length us, event | category | flops | bytes accessed | tf_op | source)
XLA Modules:
  0.0 476.1 jit_solution(7585890570126157721)
XLA Ops:
  12.3 4.1 collective-permute-start
  18.6 6.2 %collective-permute-done = bf16[24,3712]{1,0:T(8,128)(2,1)S(1)} collective-permute-done((bf16[24,3712]{1,0:T(8,128)(2,1)S(1)}, bf16[24,3712]{1,0:T(8,128)(2,1)S(1)}, u32[]{:S(2)}, u32[]{:S(2)}) %collective-permute-start) | collective-permute-done | bytes 178208 | tf_op jit(solution)/shard_map/ppermute | solution.py:1113
  26.1 13.8 %collective-permute-done.1 = bf16[2,24,3712]{2,1,0:T(8,128)(2,1)S(1)} collective-permute-done((bf16[2,24,3712]{2,1,0:T(8,128)(2,1)S(1)}, bf16[2,24,3712]{2,1,0:T(8,128)(2,1)S(1)}, u32[]{:S(2)}, u32[]{:S(2)}) %collective-permute-start.1) | collective-permute-done | bytes 356384 | tf_op jit(solution)/shard_map/ppermute | solution.py:1113
  43.3 8.7 %cosine_select_fusion.pos_ref = f32[1024,512]{1,0:T(8,128)} fusion(f32[512]{0:T(512)S(1)} %fusion.58, pred[512]{0:T(512)(128)(4,1)S(1)} %fusion.53), kind=kLoop, calls=%fused_computation.12 | loop fusion | flops 1048576 | bytes 2099712 | tf_op jit(solution)/shard_map/jit(_where)/select_n | solution.py:1091
  52.0 4.4 collective-permute-done.2
  56.6 2.5 collective-permute-start.7
  60.2 15.1 %collective-permute-done.7 = bf16[2,2,2,24,1920]{4,3,2,1,0:T(8,128)(2,1)S(1)} collective-permute-done((bf16[2,2,2,24,1920]{4,3,2,1,0:T(8,128)(2,1)S(1)}, bf16[2,2,2,24,1920]{4,3,2,1,0:T(8,128)(2,1)S(1)}, u32[]{:S(2)}, u32[]{:S(2)}) %collective-permute-start.7) | collective-permute-done | bytes 737312 | tf_op jit(solution)/shard_map/ppermute | solution.py:1113
  76.5 2.2 collective-permute-start.4
  78.7 2.3 collective-permute-done.5
  82.6 2.1 bitcast_select_fusion
  85.1 2.4 collective-permute-done.4
  88.6 4.9 %enc_qkv.1.q_ref.k_ref.v_ref = bf16[256,2304]{1,0:T(8,128)(2,1)} custom-call(bf16[256,768]{1,0:T(8,128)(2,1)} %x_ref.5, f32[16,768]{1,0:T(8,128)} %copy.82.vec_ref, bf16[768,3712]{1,0:T(8,128)(2,1)} %copy-done), custom_call_target="tpu_custom_call" | custom-call | flops 1048576 | bytes 65536 | tf_op jit(solution)/shard_map/enc_qkv/pallas_call | solution.py:367
  93.4 9.7 %collective-permute-done.9 = bf16[2,16,2176]{2,1,0:T(8,128)(2,1)S(1)} collective-permute-done((bf16[2,16,2176]{2,1,0:T(8,128)(2,1)S(1)}, bf16[2,16,2176]{2,1,0:T(8,128)(2,1)S(1)}, u32[]{:S(2)}, u32[]{:S(2)}) %collective-permute-start.9) | collective-permute-done | bytes 139296 | tf_op jit(solution)/shard_map/ppermute | solution.py:1113
  105.7 7.1 %attend.2 = (bf16[256,768]{1,0:T(8,128)(2,1)}, f32[256,768]{1,0:T(8,128)}, bf16[3,1,2,128,1024]{4,3,2,1,0:T(8,128)(2,1)}) custom-call(s32[1,256]{1,0:T(1,128)} %seg_ref.7, bf16[256,2304]{1,0:T(8,128)(2,1)} %enc_qkv.1.q_ref.k_ref.v_ref, bf16[256,2304]{1,0:T(8,128)(2,1)} %enc_qkv.1.q_ref.k_ref.v_ref, bf16[256,2304]{1,0:T(8,128)(2,1)} %enc_qkv.1.q_ref.k_ref.v_ref, ...), custom_call_target="tpu_custom_call" | custom-call | flops 1048576 | bytes 65536 | tf_op jit(solution)/shard_map/attend/pallas_call | solution.py:171
  116.7 13.0 %enc_mid.1 = (f32[256,768]{1,0:T(8,128)}, f32[256,768]{1,0:T(8,128)}, bf16[256,768]{1,0:T(8,128)(2,1)}, bf16[256,3072]{1,0:T(8,128)(2,1)}, f32[256,3072]{1,0:T(8...) custom-call(bf16[256,768]{1,0:T(8,128)(2,1)} %x_ref.5, bf16[256,768]{1,0:T(8,128)(2,1)} %get-tuple-element.148.att_ref.o_ref, ...), custom_call_target="tpu_custom_call" | custom-call | flops 1048576 | bytes 65536 | tf_op jit(solution)/shard_map/enc_mid/pallas_call | solution.py:446
  130.7 3.6 collective-permute-start.13
  138.2 3.6 collective-permute-done.12
  141.8 12.3 %collective-permute-done.13 = bf16[256,512]{1,0:T(8,128)(2,1)S(1)} collective-permute-done((bf16[256,512]{1,0:T(8,128)(2,1)S(1)}, bf16[256,512]{1,0:T(8,128)(2,1)S(1)}, u32[]{:S(2)}, u32[]{:S(2)}) %collective-permute-start.13) | collective-permute-done | bytes 262176 | tf_op jit(solution)/shard_map/ppermute | solution.py:1160
  158.9 7.8 %dec_in.1 = (f32[1024,512]{1,0:T(8,128)}, bf16[1024,1536]{1,0:T(8,128)(2,1)}) custom-call(s32[1,8]{1,0:T(1,128)} %order_ref.3, s32[1]{0:T(128)} %bitcast.line_ref, s32[1]{0:T(128)} %bitcast.1.core_ref, bf16[4,256,512]{2,1,0:T(8,128)(2,1)} %copy-done.1, bf16[4,256,512]{2,1,0:T(8,128)(2,1)} %copy-done.1, bf16[4,256,512]{2,1,0:T(8,128)(2,1)} %copy-done.2, ...), custom_call_target="tpu_custom_call" | custom-call | flops 1048576 | bytes 65536 | tf_op jit(solution)/shard_map/dec_in/pallas_call | solution.py:786
  166.8 30.8 %attend.3 = (bf16[1024,512]{1,0:T(8,128)(2,1)}, f32[1024,512]{1,0:T(8,128)}, bf16[2,4,8,128,2048]{4,3,2,1,0:T(8,128)(2,1)}) custom-call(s32[1,1024]{1,0:T(1,128)} %seg_ref.6, bf16[1024,1536]{1,0:T(8,128)(2,1)} %get-tuple-element.161.q_ref.k_ref.v_ref, bf16[1024,1536]{1,0:T(8,128)(2,1)} %get-tuple-element.161.q_ref.k_ref.v_ref, ...), custom_call_target="tpu_custom_call" | custom-call | flops 1048576 | bytes 65536 | tf_op jit(solution)/shard_map/attend/pallas_call | solution.py:171
  197.5 2.1 all-gather.5.cloned.1.call-done.up_ref.down_ref
  199.6 28.2 %dec_mid.1 = (bf16[1024,512]{1,0:T(8,128)(2,1)}, f32[1024,512]{1,0:T(8,128)}, bf16[1024,512]{1,0:T(8,128)(2,1)}, bf16[512,4608]{1,0:T(8,128)(2,1)}, f32[4,1,512]{2,1,0:T(1,128)}, /*index=5*/f32[8,512]{1,0:T(8,128)}) custom-call(f32[1024,512]{1,0:T(8,128)} %get-tuple-element.160.x_ref, bf16[1024,512]{1,0:T(8,128)(2,1)} %get-tuple-element.162.att_ref.o_ref, ...), custom_call_target="tpu_custom_call" | custom-call | flops 1048576 | bytes 65536 | tf_op jit(solution)/shard_map/dec_mid/pallas_call | solution.py:920
  230.1 37.2 %attend_back.2 = (bf16[1024,512]{1,0:T(8,128)(2,1)}, bf16[1024,512]{1,0:T(8,128)(2,1)}, bf16[1024,512]{1,0:T(8,128)(2,1)}) custom-call(s32[1,1024]{1,0:T(1,128)} %seg_ref.6, bf16[1024,1536]{1,0:T(8,128)(2,1)} %get-tuple-element.161.q_ref.k_ref.v_ref, bf16[1024,1536]{1,0:T(8,128)(2,1)} %get-tuple-element.161.q_ref.k_ref.v_ref, ...), custom_call_target="tpu_custom_call" | custom-call | flops 1048576 | bytes 65536 | tf_op jit(solution)/shard_map/attend_back/pallas_call | solution.py:282
  267.3 9.1 %dec_back.1 = (f32[16,512]{1,0:T(8,128)}, bf16[4,256,512]{2,1,0:T(8,128)(2,1)}, bf16[4,256,512]{2,1,0:T(8,128)(2,1)}) custom-call(s32[1,8]{1,0:T(1,128)} %order_ref.3, s32[1]{0:T(128)} %bitcast.1.core_ref, f32[1024,512]{1,0:T(8,128)} %get-tuple-element.160.x_ref, bf16[1024,512]{1,0:T(8,128)(2,1)} %get-tuple-element.172.dq_ref, ...), custom_call_target="tpu_custom_call" | custom-call | flops 1048576 | bytes 65536 | tf_op jit(solution)/shard_map/dec_back/pallas_call | solution.py:1030
  276.4 4.1 collective-permute-start.17
  280.4 2.5 collective-permute-done.17
  285.1 8.0 %collective-permute-start.19 = (bf16[256,512]{1,0:T(8,128)(2,1)S(1)}, bf16[256,512]{1,0:T(8,128)(2,1)S(1)}, u32[]{:S(2)}, u32[]{:S(2)}) collective-permute-start(bf16[256,512]{1,0:T(8,128)(2,1)S(1)} %get-tuple-element.298), channel_id=1, source_target_pairs={{0,4},{1,5},{2,6},{3,7},{4,0},{5,1},{6,2},{7,3},{8,12},{9,13},{10,... | collective-permute-start | bytes 786440 | tf_op jit(solution)/shard_map/ppermute | solution.py:1160
  293.1 2.8 collective-permute-start.20
  296.0 6.7 %dec_grad.1 = bf16[512,1664]{1,0:T(8,128)(2,1)} custom-call(f32[1024,512]{1,0:T(8,128)} %get-tuple-element.160.x_ref, bf16[1024,512]{1,0:T(8,128)(2,1)} %get-tuple-element.172.dq_ref, bf16[1024,512]{1,0:T(8,128)(2,1)} %get-tuple-element.173.dk_ref, bf16[1024,512]{1,0:T(8,128)(2,1)} %get-tuple-element.174.dv_ref, f32[16,512]{1,0:T(8,128)} %copy-done.18, ...), custom_call_target="tpu_custom_call" | custom-call | flops 1048576 | bytes 65536 | tf_op jit(solution)/shard_map/dec_grad/pallas_call | solution.py:1073
  302.6 6.2 %collective-permute-done.19 = bf16[256,512]{1,0:T(8,128)(2,1)S(1)} collective-permute-done((bf16[256,512]{1,0:T(8,128)(2,1)S(1)}, bf16[256,512]{1,0:T(8,128)(2,1)S(1)}, u32[]{:S(2)}, u32[]{:S(2)}) %collective-permute-start.19) | collective-permute-done | bytes 262176 | tf_op jit(solution)/shard_map/ppermute | solution.py:1160
  310.9 17.1 %enc_mid_back.1 = (bf16[16,24,1280]{2,1,0:T(8,128)(2,1)}, bf16[16,24,1280]{2,1,0:T(8,128)(2,1)}, bf16[16,24,3072]{2,1,0:T(8,128)(2,1)}, bf16[16,24,3072]{2,1,0:T...) custom-call(s32[1]{0:T(128)} %bitcast.1.core_ref, ...), custom_call_target="tpu_custom_call" | custom-call | flops 1048576 | bytes 65536 | tf_op jit(solution)/shard_map/enc_mid_back/pallas_call | solution.py:621
  328.1 2.1 copy.93
  332.4 16.1 %reduce-scatter.6.cloned.1.call-done = bf16[128,1664]{1,0:T(8,128)(2,1)} async-done(((bf16[512,1664]{1,0:T(8,128)(2,1)}), bf16[128,1664]{1,0:T(8,128)(2,1)}) %reduce-scatter.6.cloned.1.call-update) | async-done | bytes 426000 | tf_op jit(solution)/shard_map/reduce_scatter | solution.py:1471
  348.6 2.3 pad_maximum_fusion.1
  354.8 2.4 fusion.1
  364.1 7.9 %attend_back.3 = (bf16[256,768]{1,0:T(8,128)(2,1)}, bf16[256,768]{1,0:T(8,128)(2,1)}, bf16[256,768]{1,0:T(8,128)(2,1)}) custom-call(s32[1,256]{1,0:T(1,128)} %seg_ref.7, bf16[256,2304]{1,0:T(8,128)(2,1)} %enc_qkv.1.q_ref.k_ref.v_ref, bf16[256,2304]{1,0:T(8,128)(2,1)} %enc_qkv.1.q_ref.k_ref.v_ref, bf16[256,2304]{1,0:T(8,128)(2,1)} %enc_qkv.1.q_ref.k_ref.v_ref, ...), custom_call_target="tpu_custom_call" | custom-call | flops 1048576 | bytes 65536 | tf_op jit(solution)/shard_map/attend_back/pallas_call | solution.py:282
  372.0 6.9 %enc_qkv_back.1 = (bf16[256,768]{1,0:T(8,128)(2,1)}, bf16[16,24,1152]{2,1,0:T(8,128)(2,1)}, bf16[16,24,1280]{2,1,0:T(8,128)(2,1)}, bf16[16,24,1152]{2,1,0:T(8,128)(2,1)}, bf16[16,24,1280]{2,1,0:T(8,128)(2,1)}) custom-call(s32[1]{0:T(128)} %bitcast.1.core_ref, bf16[256,768]{1,0:T(8,128)(2,1)} %x_ref.5, bf16[256,768]{1,0:T(8,128)(2,1)} %get-tuple-element.214.dq_ref, ...), custom_call_target="tpu_custom_call" | custom-call | flops 1048576 | bytes 65536 | tf_op jit(solution)/shard_map/enc_qkv_back/pallas_call | solution.py:727
  378.9 1.9 constant_dynamic-slice_fusion.7
  382.6 2.4 collective-permute-done.26
  385.1 2.8 collective-permute-done.24
  393.9 2.0 collective-permute-start.29
  399.2 12.1 %collective-permute-done.31 = bf16[2,2,24,1280]{3,2,1,0:T(8,128)(2,1)S(1)} collective-permute-done((bf16[2,2,24,1280]{3,2,1,0:T(8,128)(2,1)S(1)}, bf16[2,2,24,1280]{3,2,1,0:T(8,128)(2,1)S(1)}, u32[]{:S(2)}, u32[]{:S(2)}) %collective-permute-start.31) | collective-permute-done | bytes 245792 | tf_op jit(solution)/shard_map/ppermute | solution.py:1113
  413.2 2.1 fusion.4
  427.7 4.0 collective-permute-done.35
  438.2 3.5 collective-permute-start.40
  449.8 3.2 collective-permute-done.40
  453.0 4.0 collective-permute-done.39
  459.8 4.9 %collective-permute-done.41 = bf16[24,2432]{1,0:T(8,128)(2,1)} collective-permute-done((bf16[24,2432]{1,0:T(8,128)(2,1)}, bf16[24,2432]{1,0:T(8,128)(2,1)}, u32[]{:S(2)}, u32[]{:S(2)}) %collective-permute-start.41) | collective-permute-done | bytes 116768 | tf_op jit(solution)/shard_map/ppermute | solution.py:1113
  (284 shorter events, 99.7 us)
Async XLA Ops:
  7.2 109.5 %all-gather.3.cloned.1.call-start = ((), (), s32[]{:S(2)}) async-start(), calls=%async_computation.3 | async-start | bytes 9732096 | tf_op jit(solution)/shard_map/all_gather | solution.py:1351
  9.0 190.6 %all-gather.5.cloned.1.call-start = ((), (), s32[]{:S(2)}) async-start(), calls=%async_computation.4 | async-start | bytes 4325376 | tf_op jit(solution)/shard_map/all_gather | solution.py:1396
  12.3 12.4 %collective-permute-start = (bf16[24,3712]{1,0:T(8,128)(2,1)S(1)}, bf16[24,3712]{1,0:T(8,128)(2,1)S(1)}, u32[]{:S(2)}, u32[]{:S(2)}) collective-permute-start(bf16[24,3712]{1,0:T(8,128)(2,1)S(1)} %pad_maximum_fusion.3), channel_id=1, source_target_pairs={{0,4},{1,5},{2,6},{3,7},{4,0},{5,1},{6,2},{7,3},{8,12},{9,13},{10,... | collective-permute-start | bytes 534536 | tf_op jit(solution)/shard_map/ppermute | solution.py:1113
  24.9 15.0 %collective-permute-start.1 = (bf16[2,24,3712]{2,1,0:T(8,128)(2,1)S(1)}, bf16[2,24,3712]{2,1,0:T(8,128)(2,1)S(1)}, u32[]{:S(2)}, u32[]{:S(2)}) collective-permute-start(bf16[2,24,3712]{2,1,0:T(8,128)(2,1)S(1)} %broadcast_select_fusion.7), channel_id=1, source_target_pairs={{0,2},{1,3},{2,0},{3,1},{4,6},{5,7},{6,4},{7,5},{8,10},{9,11},{10,... | collective-permute-start | bytes 1069064 | tf_op jit(solution)/shard_map/ppermute | solution.py:1113
  40.3 16.1 %collective-permute-start.2 = (bf16[2,2,24,1792]{3,2,1,0:T(8,128)(2,1)S(1)}, bf16[2,2,24,1792]{3,2,1,0:T(8,128)(2,1)S(1)}, u32[]{:S(2)}, u32[]{:S(2)}) collective-permute-start(bf16[2,2,24,1792]{3,2,1,0:T(8,128)(2,1)S(1)} %slice.172), channel_id=1, source_target_pairs={{0,8},{8,0},{16,24},{24,16},{1,9},{9,1},{17,25},{25,17},{2,10},{10... | collective-permute-start | bytes 1032200 | tf_op jit(solution)/shard_map/ppermute | solution.py:1113
  41.8 14.6 %collective-permute-start.6 = (bf16[2,2,24,1920]{3,2,1,0:T(8,128)(2,1)S(1)}, bf16[2,2,24,1920]{3,2,1,0:T(8,128)(2,1)S(1)}, u32[]{:S(2)}, u32[]{:S(2)}) collective-permute-start(bf16[2,2,24,1920]{3,2,1,0:T(8,128)(2,1)S(1)} %slice.173), channel_id=1, source_target_pairs={{0,16},{8,24},{16,0},{24,8},{1,17},{9,25},{17,1},{25,9},{2,18},{10... | collective-permute-start | bytes 1105928 | tf_op jit(solution)/shard_map/ppermute | solution.py:1113
  56.6 18.7 %collective-permute-start.7 = (bf16[2,2,2,24,1920]{4,3,2,1,0:T(8,128)(2,1)S(1)}, bf16[2,2,2,24,1920]{4,3,2,1,0:T(8,128)(2,1)S(1)}, u32[]{:S(2)}, u32[]{:S(2)}) collective-permute-start(bf16[2,2,2,24,1920]{4,3,2,1,0:T(8,128)(2,1)S(1)} %broadcast_select_fusion.3), channel_id=1, source_target_pairs={{0,8},{8,0},{16,24},{24,16},{1,9},{9,1},{17,25},{25,17},{2,10},{10... | collective-permute-start | bytes 2211848 | tf_op jit(solution)/shard_map/ppermute | solution.py:1113
  59.3 16.3 %collective-permute-start.3 = (bf16[2,2,2,24,1792]{4,3,2,1,0:T(8,128)(2,1)S(1)}, bf16[2,2,2,24,1792]{4,3,2,1,0:T(8,128)(2,1)S(1)}, u32[]{:S(2)}, u32[]{:S(2)}) collective-permute-start(bf16[2,2,2,24,1792]{4,3,2,1,0:T(8,128)(2,1)S(1)} %broadcast_select_fusion.5), channel_id=1, source_target_pairs={{0,16},{8,24},{16,0},{24,8},{1,17},{9,25},{17,1},{25,9},{2,18},{10... | collective-permute-start | bytes 2064392 | tf_op jit(solution)/shard_map/ppermute | solution.py:1113
  75.5 7.1 %collective-permute-start.8 = (bf16[2,2,2,2,24,1920]{5,4,3,2,1,0:T(8,128)(2,1)S(1)}, bf16[2,2,2,2,24,1920]{5,4,3,2,1,0:T(8,128)(2,1)}, u32[]{:S(2)}, u32[]{:S(2)}) collective-permute-start(bf16[2,2,2,2,24,1920]{5,4,3,2,1,0:T(8,128)(2,1)S(1)} %broadcast_select_fusion), channel_id=1, source_target_pairs={{0,1},{1,0},{2,3},{3,2},{4,5},{5,4},{6,7},{7,6},{8,9},{9,8},{10,11... | collective-permute-start | bytes 4423688 | tf_op jit(solution)/shard_map/ppermute | solution.py:1113
  75.8 5.2 %collective-permute-start.5 = (bf16[2,2,2,2,24,1792]{5,4,3,2,1,0:T(8,128)(2,1)S(1)}, bf16[2,2,2,2,24,1792]{5,4,3,2,1,0:T(8,128)(2,1)}, u32[]{:S(2)}, u32[]{:S(2)}) collective-permute-start(bf16[2,2,2,2,24,1792]{5,4,3,2,1,0:T(8,128)(2,1)S(1)} %broadcast_select_fusion.1), channel_id=1, source_target_pairs={{0,1},{1,0},{2,3},{3,2},{4,5},{5,4},{6,7},{7,6},{8,9},{9,8},{10,11... | collective-permute-start | bytes 4128776 | tf_op jit(solution)/shard_map/ppermute | solution.py:1113
  76.5 11.0 %collective-permute-start.4 = (bf16[16,2176]{1,0:T(8,128)(2,1)S(1)}, bf16[16,2176]{1,0:T(8,128)(2,1)S(1)}, u32[]{:S(2)}, u32[]{:S(2)}) collective-permute-start(bf16[16,2176]{1,0:T(8,128)(2,1)S(1)} %pad_maximum_fusion.4), channel_id=1, source_target_pairs={{0,4},{1,5},{2,6},{3,7},{4,0},{5,1},{6,2},{7,3},{8,12},{9,13},{10,... | collective-permute-start | bytes 208904 | tf_op jit(solution)/shard_map/ppermute | solution.py:1113
  87.7 15.4 %collective-permute-start.9 = (bf16[2,16,2176]{2,1,0:T(8,128)(2,1)S(1)}, bf16[2,16,2176]{2,1,0:T(8,128)(2,1)S(1)}, u32[]{:S(2)}, u32[]{:S(2)}) collective-permute-start(bf16[2,16,2176]{2,1,0:T(8,128)(2,1)S(1)} %broadcast_select_fusion.9), channel_id=1, source_target_pairs={{0,2},{1,3},{2,0},{3,1},{4,6},{5,7},{6,4},{7,5},{8,10},{9,11},{10,... | collective-permute-start | bytes 417800 | tf_op jit(solution)/shard_map/ppermute | solution.py:1113
  103.3 9.6 %collective-permute-start.10 = (bf16[2,2,16,2176]{3,2,1,0:T(8,128)(2,1)S(1)}, bf16[2,2,16,2176]{3,2,1,0:T(8,128)(2,1)S(1)}, u32[]{:S(2)}, u32[]{:S(2)}) collective-permute-start(bf16[2,2,16,2176]{3,2,1,0:T(8,128)(2,1)S(1)} %broadcast_select_fusion.8), channel_id=1, source_target_pairs={{0,16},{8,24},{16,0},{24,8},{1,17},{9,25},{17,1},{25,9},{2,18},{10... | collective-permute-start | bytes 835592 | tf_op jit(solution)/shard_map/ppermute | solution.py:1113
  113.0 16.8 %collective-permute-start.11 = (bf16[2,2,2,16,2176]{4,3,2,1,0:T(8,128)(2,1)S(1)}, bf16[2,2,2,16,2176]{4,3,2,1,0:T(8,128)(2,1)S(1)}, u32[]{:S(2)}, u32[]{:S(2)}) collective-permute-start(bf16[2,2,2,16,2176]{4,3,2,1,0:T(8,128)(2,1)S(1)} %broadcast_select_fusion.6), channel_id=1, source_target_pairs={{0,8},{8,0},{16,24},{24,16},{1,9},{9,1},{17,25},{25,17},{2,10},{10... | collective-permute-start | bytes 1671176 | tf_op jit(solution)/shard_map/ppermute | solution.py:1113
  129.8 179.0 %reduce-scatter.4.cloned.1.call-start = ((), (), s32[]{:S(2)}) async-start(), calls=%async_computation.5 | async-start | bytes 5898240 | tf_op jit(solution)/shard_map/reduce_scatter | solution.py:1431
  130.1 5.3 %collective-permute-start.15 = (bf16[2,2,2,2,16,2176]{5,4,3,2,1,0:T(8,128)(2,1)S(1)}, bf16[2,2,2,2,16,2176]{5,4,3,2,1,0:T(8,128)(2,1)S(1)}, u32[]{:S(2)}, u32[]{:S(2)}) collective-permute-start(bf16[2,2,2,2,16,2176]{5,4,3,2,1,0:T(8,128)(2,1)S(1)} %broadcast_select_fusion.2), channel_id=1, source_target_pairs={{0,1},{1,0},{2,3},{3,2},{4,5},{5,4},{6,7},{7,6},{8,9},{9,8},{10,11... | collective-permute-start | bytes 3342344 | tf_op jit(solution)/shard_map/ppermute | solution.py:1113
  130.7 11.1 %collective-permute-start.12 = (bf16[256,512]{1,0:T(8,128)(2,1)S(1)}, bf16[256,512]{1,0:T(8,128)(2,1)S(1)}, u32[]{:S(2)}, u32[]{:S(2)}) collective-permute-start(bf16[256,512]{1,0:T(8,128)(2,1)S(1)} %copy-done.26), channel_id=1, source_target_pairs={{0,2},{1,3},{2,4},{3,5},{4,6},{5,7},{6,0},{7,1},{8,10},{9,11},{10,... | collective-permute-start | bytes 786440 | tf_op jit(solution)/shard_map/ppermute | solution.py:1160
  130.7 23.4 %collective-permute-start.13 = (bf16[256,512]{1,0:T(8,128)(2,1)S(1)}, bf16[256,512]{1,0:T(8,128)(2,1)S(1)}, u32[]{:S(2)}, u32[]{:S(2)}) collective-permute-start(bf16[256,512]{1,0:T(8,128)(2,1)S(1)} %copy-done.26), channel_id=1, source_target_pairs={{0,4},{1,5},{2,6},{3,7},{4,0},{5,1},{6,2},{7,3},{8,12},{9,13},{10,... | collective-permute-start | bytes 786440 | tf_op jit(solution)/shard_map/ppermute | solution.py:1160
  134.3 19.9 %collective-permute-start.14 = (bf16[256,512]{1,0:T(8,128)(2,1)S(1)}, bf16[256,512]{1,0:T(8,128)(2,1)}, u32[]{:S(2)}, u32[]{:S(2)}) collective-permute-start(bf16[256,512]{1,0:T(8,128)(2,1)S(1)} %copy-done.26), channel_id=1, source_target_pairs={{0,6},{1,7},{2,0},{3,1},{4,2},{5,3},{6,4},{7,5},{8,14},{9,15},{10,... | collective-permute-start | bytes 786440 | tf_op jit(solution)/shard_map/ppermute | solution.py:1160
  155.2 2.7 collective-permute-start.16
  227.9 120.7 %reduce-scatter.6.cloned.1.call-start = ((), (), s32[]{:S(2)}) async-start(), calls=%async_computation.6 | async-start | bytes 2129920 | tf_op jit(solution)/shard_map/reduce_scatter | solution.py:1471
  276.4 6.6 %collective-permute-start.17 = (bf16[4,256,512]{2,1,0:T(8,128)(2,1)}, bf16[4,256,512]{2,1,0:T(8,128)(2,1)S(1)}, u32[]{:S(2)}, u32[]{:S(2)}) collective-permute-start(bf16[4,256,512]{2,1,0:T(8,128)(2,1)} %get-tuple-element.178), channel_id=1, source_target_pairs={{0,1},{1,0},{2,3},{3,2},{4,5},{5,4},{6,7},{7,6},{8,9},{9,8},{10,11... | collective-permute-start | bytes 3145736 | tf_op jit(solution)/shard_map/ppermute | solution.py:1113
  284.3 18.3 %collective-permute-start.18 = (bf16[256,512]{1,0:T(8,128)(2,1)S(1)}, bf16[256,512]{1,0:T(8,128)(2,1)S(1)}, u32[]{:S(2)}, u32[]{:S(2)}) collective-permute-start(bf16[256,512]{1,0:T(8,128)(2,1)S(1)} %get-tuple-element.299), channel_id=1, source_target_pairs={{0,2},{1,3},{2,4},{3,5},{4,6},{5,7},{6,0},{7,1},{8,10},{9,11},{10,... | collective-permute-start | bytes 786440 | tf_op jit(solution)/shard_map/ppermute | solution.py:1160
  285.1 23.7 %collective-permute-start.19 = (bf16[256,512]{1,0:T(8,128)(2,1)S(1)}, bf16[256,512]{1,0:T(8,128)(2,1)S(1)}, u32[]{:S(2)}, u32[]{:S(2)}) collective-permute-start(bf16[256,512]{1,0:T(8,128)(2,1)S(1)} %get-tuple-element.298), channel_id=1, source_target_pairs={{0,4},{1,5},{2,6},{3,7},{4,0},{5,1},{6,2},{7,3},{8,12},{9,13},{10,... | collective-permute-start | bytes 786440 | tf_op jit(solution)/shard_map/ppermute | solution.py:1160
  293.1 15.7 %collective-permute-start.20 = (bf16[256,512]{1,0:T(8,128)(2,1)S(1)}, bf16[256,512]{1,0:T(8,128)(2,1)S(1)}, u32[]{:S(2)}, u32[]{:S(2)}) collective-permute-start(bf16[256,512]{1,0:T(8,128)(2,1)S(1)} %get-tuple-element.297), channel_id=1, source_target_pairs={{0,6},{1,7},{2,0},{3,1},{4,2},{5,3},{6,4},{7,5},{8,14},{9,15},{10,... | collective-permute-start | bytes 786440 | tf_op jit(solution)/shard_map/ppermute | solution.py:1160
  308.8 80.4 %reduce-scatter.8.cloned.1.call-start = ((), (), s32[]{:S(2)}) async-start(), calls=%async_computation.7 | async-start | bytes 1806336 | tf_op jit(solution)/shard_map/reduce_scatter | solution.py:1492
  330.2 24.5 %collective-permute-start.21 = (bf16[2,2,2,2,24,3072]{5,4,2,3,1,0:T(8,128)(2,1)S(1)}, bf16[2,2,2,2,24,3072]{5,4,2,3,1,0:T(8,128)(2,1)}, u32[]{:S(2)}, u32[]{:S(2)}) collective-permute-start(bf16[2,2,2,2,24,3072]{5,4,2,3,1,0:T(8,128)(2,1)S(1)} %copy.93), channel_id=1, source_target_pairs={{0,1},{1,0},{2,3},{3,2},{4,5},{5,4},{6,7},{7,6},{8,9},{9,8},{10,11... | collective-permute-start | bytes 7077896 | tf_op jit(solution)/shard_map/ppermute | solution.py:1113
  332.3 22.5 %collective-permute-start.22 = (bf16[2,2,2,2,24,3072]{5,4,2,3,1,0:T(8,128)(2,1)}, bf16[2,2,2,2,24,3072]{5,4,2,3,1,0:T(8,128)(2,1)}, u32[]{:S(2)}, u32[]{:S(2)}) collective-permute-start(bf16[2,2,2,2,24,3072]{5,4,2,3,1,0:T(8,128)(2,1)} %copy.94), channel_id=1, source_target_pairs={{0,1},{1,0},{2,3},{3,2},{4,5},{5,4},{6,7},{7,6},{8,9},{9,8},{10,11... | collective-permute-start | bytes 7077896 | tf_op jit(solution)/shard_map/ppermute | solution.py:1113
  350.9 3.9 collective-permute-start.23
  359.5 28.4 %collective-permute-start.24 = (bf16[2,2,2,24,3072]{4,3,1,2,0:T(8,128)(2,1)S(1)}, bf16[2,2,2,24,3072]{4,3,1,2,0:T(8,128)(2,1)S(1)}, u32[]{:S(2)}, u32[]{:S(2)}) collective-permute-start(bf16[2,2,2,24,3072]{4,3,1,2,0:T(8,128)(2,1)S(1)} %fusion), channel_id=1, source_target_pairs={{0,16},{8,24},{16,0},{24,8},{1,17},{9,25},{17,1},{25,9},{2,18},{10... | collective-permute-start | bytes 3538952 | tf_op jit(solution)/shard_map/ppermute | solution.py:1113
  360.8 28.2 %collective-permute-start.25 = (bf16[2,2,2,24,3072]{4,3,1,2,0:T(8,128)(2,1)S(1)}, bf16[2,2,2,24,3072]{4,3,1,2,0:T(8,128)(2,1)}, u32[]{:S(2)}, u32[]{:S(2)}) collective-permute-start(bf16[2,2,2,24,3072]{4,3,1,2,0:T(8,128)(2,1)S(1)} %fusion.1), channel_id=1, source_target_pairs={{0,8},{8,0},{16,24},{24,16},{1,9},{9,1},{17,25},{25,17},{2,10},{10... | collective-permute-start | bytes 3538952 | tf_op jit(solution)/shard_map/ppermute | solution.py:1113
  362.5 22.5 %collective-permute-start.26 = (bf16[2,2,2,24,1280]{4,3,2,1,0:T(8,128)(2,1)}, bf16[2,2,2,24,1280]{4,3,2,1,0:T(8,128)(2,1)}, u32[]{:S(2)}, u32[]{:S(2)}) collective-permute-start(bf16[2,2,2,24,1280]{4,3,2,1,0:T(8,128)(2,1)} %fusion.20), channel_id=1, source_target_pairs={{0,2},{1,3},{2,0},{3,1},{4,6},{5,7},{6,4},{7,5},{8,10},{9,11},{10,... | collective-permute-start | bytes 1474568 | tf_op jit(solution)/shard_map/ppermute | solution.py:1113
  390.8 20.5 %collective-permute-start.30 = (bf16[2,2,24,3072]{3,2,0,1:T(8,128)(2,1)S(1)}, bf16[2,2,24,3072]{3,2,0,1:T(8,128)(2,1)S(1)}, u32[]{:S(2)}, u32[]{:S(2)}) collective-permute-start(bf16[2,2,24,3072]{3,2,0,1:T(8,128)(2,1)S(1)} %fusion.6), channel_id=1, source_target_pairs={{0,16},{8,24},{16,0},{24,8},{1,17},{9,25},{17,1},{25,9},{2,18},{10... | collective-permute-start | bytes 1769480 | tf_op jit(solution)/shard_map/ppermute | solution.py:1113
  392.4 18.8 %collective-permute-start.28 = (bf16[2,2,2,2,24,1280]{5,4,2,3,1,0:T(8,128)(2,1)S(1)}, bf16[2,2,2,2,24,1280]{5,4,2,3,1,0:T(8,128)(2,1)S(1)}, u32[]{:S(2)}, u32[]{:S(2)}) collective-permute-start(bf16[2,2,2,2,24,1280]{5,4,2,3,1,0:T(8,128)(2,1)S(1)} %copy.100), channel_id=1, source_target_pairs={{0,1},{1,0},{2,3},{3,2},{4,5},{5,4},{6,7},{7,6},{8,9},{9,8},{10,11... | collective-permute-start | bytes 2949128 | tf_op jit(solution)/shard_map/ppermute | solution.py:1113
  393.9 17.4 %collective-permute-start.29 = (bf16[2,2,24,3072]{3,2,0,1:T(8,128)(2,1)S(1)}, bf16[2,2,24,3072]{3,2,0,1:T(8,128)(2,1)S(1)}, u32[]{:S(2)}, u32[]{:S(2)}) collective-permute-start(bf16[2,2,24,3072]{3,2,0,1:T(8,128)(2,1)S(1)} %fusion.7), channel_id=1, source_target_pairs={{0,8},{8,0},{16,24},{24,16},{1,9},{9,1},{17,25},{25,17},{2,10},{10... | collective-permute-start | bytes 1769480 | tf_op jit(solution)/shard_map/ppermute | solution.py:1113
  396.0 15.2 %collective-permute-start.27 = (bf16[2,2,2,2,24,1152]{5,4,2,3,1,0:T(8,128)(2,1)S(1)}, bf16[2,2,2,2,24,1152]{5,4,2,3,1,0:T(8,128)(2,1)S(1)}, u32[]{:S(2)}, u32[]{:S(2)}) collective-permute-start(bf16[2,2,2,2,24,1152]{5,4,2,3,1,0:T(8,128)(2,1)S(1)} %copy.99), channel_id=1, source_target_pairs={{0,1},{1,0},{2,3},{3,2},{4,5},{5,4},{6,7},{7,6},{8,9},{9,8},{10,11... | collective-permute-start | bytes 2654216 | tf_op jit(solution)/shard_map/ppermute | solution.py:1113
  397.6 13.7 %collective-permute-start.31 = (bf16[2,2,24,1280]{3,2,1,0:T(8,128)(2,1)S(1)}, bf16[2,2,24,1280]{3,2,1,0:T(8,128)(2,1)S(1)}, u32[]{:S(2)}, u32[]{:S(2)}) collective-permute-start(bf16[2,2,24,1280]{3,2,1,0:T(8,128)(2,1)S(1)} %fusion.24), channel_id=1, source_target_pairs={{0,4},{1,5},{2,6},{3,7},{4,0},{5,1},{6,2},{7,3},{8,12},{9,13},{10,... | collective-permute-start | bytes 737288 | tf_op jit(solution)/shard_map/ppermute | solution.py:1113
  416.3 19.9 %copy-start.22 = (bf16[1,1,2,2,24,1152]{5,4,3,2,1,0:T(8,128)(2,1)S(1)}, bf16[1,1,2,2,24,1152]{5,4,3,2,1,0:T(8,128)(2,1)}, u32[]{:S(2)}) copy-start(bf16[1,1,2,2,24,1152]{5,4,3,2,1,0:T(8,128)(2,1)} %get-tuple-element.303) | copy-start | bytes 663556
  416.3 15.5 %collective-permute-start.34 = (bf16[2,24,6144]{2,1,0:T(8,128)(2,1)}, bf16[2,24,6144]{2,1,0:T(8,128)(2,1)S(1)}, u32[]{:S(2)}, u32[]{:S(2)}) collective-permute-start(bf16[2,24,6144]{2,1,0:T(8,128)(2,1)} %fusion.8), channel_id=1, source_target_pairs={{0,2},{1,3},{2,0},{3,1},{4,6},{5,7},{6,4},{7,5},{8,10},{9,11},{10,... | collective-permute-start | bytes 1769480 | tf_op jit(solution)/shard_map/ppermute | solution.py:1113
  416.3 15.4 %collective-permute-start.33 = (bf16[2,2,2,24,1280]{4,3,1,2,0:T(8,128)(2,1)}, bf16[2,2,2,24,1280]{4,3,1,2,0:T(8,128)(2,1)}, u32[]{:S(2)}, u32[]{:S(2)}) collective-permute-start(bf16[2,2,2,24,1280]{4,3,1,2,0:T(8,128)(2,1)} %fusion.21), channel_id=1, source_target_pairs={{0,8},{8,0},{16,24},{24,16},{1,9},{9,1},{17,25},{25,17},{2,10},{10... | collective-permute-start | bytes 1474568 | tf_op jit(solution)/shard_map/ppermute | solution.py:1113
  416.9 14.8 %collective-permute-start.32 = (bf16[2,2,2,24,1152]{4,3,1,2,0:T(8,128)(2,1)}, bf16[2,2,2,24,1152]{4,3,1,2,0:T(8,128)(2,1)}, u32[]{:S(2)}, u32[]{:S(2)}) collective-permute-start(bf16[2,2,2,24,1152]{4,3,1,2,0:T(8,128)(2,1)} %fusion.27), channel_id=1, source_target_pairs={{0,16},{8,24},{16,0},{24,8},{1,17},{9,25},{17,1},{25,9},{2,18},{10... | collective-permute-start | bytes 1327112 | tf_op jit(solution)/shard_map/ppermute | solution.py:1113
  419.6 12.1 %collective-permute-start.35 = (bf16[2,24,1280]{2,1,0:T(8,128)(2,1)}, bf16[2,24,1280]{2,1,0:T(8,128)(2,1)}, u32[]{:S(2)}, u32[]{:S(2)}) collective-permute-start(bf16[2,24,1280]{2,1,0:T(8,128)(2,1)} %fusion.33), channel_id=1, source_target_pairs={{0,16},{8,24},{16,0},{24,8},{1,17},{9,25},{17,1},{25,9},{2,18},{10... | collective-permute-start | bytes 368648 | tf_op jit(solution)/shard_map/ppermute | solution.py:1113
  433.0 8.7 %collective-permute-start.38 = (bf16[24,1280]{1,0:T(8,128)(2,1)S(1)}, bf16[24,1280]{1,0:T(8,128)(2,1)S(1)}, u32[]{:S(2)}, u32[]{:S(2)}) collective-permute-start(bf16[24,1280]{1,0:T(8,128)(2,1)S(1)} %fusion.44), channel_id=1, source_target_pairs={{0,8},{8,0},{16,24},{24,16},{1,9},{9,1},{17,25},{25,17},{2,10},{10... | collective-permute-start | bytes 184328 | tf_op jit(solution)/shard_map/ppermute | solution.py:1113
  435.6 7.8 %collective-permute-start.37 = (bf16[2,2,24,1280]{3,2,0,1:T(8,128)(2,1)S(1)}, bf16[2,2,24,1280]{3,2,0,1:T(8,128)(2,1)S(1)}, u32[]{:S(2)}, u32[]{:S(2)}) collective-permute-start(bf16[2,2,24,1280]{3,2,0,1:T(8,128)(2,1)S(1)} %fusion.23), channel_id=1, source_target_pairs={{0,16},{8,24},{16,0},{24,8},{1,17},{9,25},{17,1},{25,9},{2,18},{10... | collective-permute-start | bytes 737288 | tf_op jit(solution)/shard_map/ppermute | solution.py:1113
  437.3 6.0 %collective-permute-start.36 = (bf16[2,2,24,1152]{3,2,0,1:T(8,128)(2,1)S(1)}, bf16[2,2,24,1152]{3,2,0,1:T(8,128)(2,1)S(1)}, u32[]{:S(2)}, u32[]{:S(2)}) collective-permute-start(bf16[2,2,24,1152]{3,2,0,1:T(8,128)(2,1)S(1)} %fusion.28), channel_id=1, source_target_pairs={{0,8},{8,0},{16,24},{24,16},{1,9},{9,1},{17,25},{25,17},{2,10},{10... | collective-permute-start | bytes 663560 | tf_op jit(solution)/shard_map/ppermute | solution.py:1113
  438.2 14.8 %collective-permute-start.40 = (bf16[24,6144]{1,0:T(8,128)(2,1)S(1)}, bf16[24,6144]{1,0:T(8,128)(2,1)S(1)}, u32[]{:S(2)}, u32[]{:S(2)}) collective-permute-start(bf16[24,6144]{1,0:T(8,128)(2,1)S(1)} %fusion.16), channel_id=1, source_target_pairs={{0,4},{1,5},{2,6},{3,7},{4,0},{5,1},{6,2},{7,3},{8,12},{9,13},{10,... | collective-permute-start | bytes 884744 | tf_op jit(solution)/shard_map/ppermute | solution.py:1113
  445.7 11.3 %collective-permute-start.39 = (bf16[2,24,2432]{2,1,0:T(8,128)(2,1)S(1)}, bf16[2,24,2432]{2,1,0:T(8,128)(2,1)S(1)}, u32[]{:S(2)}, u32[]{:S(2)}) collective-permute-start(bf16[2,24,2432]{2,1,0:T(8,128)(2,1)S(1)} %fusion.34), channel_id=1, source_target_pairs={{0,2},{1,3},{2,0},{3,1},{4,6},{5,7},{6,4},{7,5},{8,10},{9,11},{10,... | collective-permute-start | bytes 700424 | tf_op jit(solution)/shard_map/ppermute | solution.py:1113
  457.7 7.0 %collective-permute-start.41 = (bf16[24,2432]{1,0:T(8,128)(2,1)}, bf16[24,2432]{1,0:T(8,128)(2,1)}, u32[]{:S(2)}, u32[]{:S(2)}) collective-permute-start(bf16[24,2432]{1,0:T(8,128)(2,1)} %fusion.38), channel_id=1, source_target_pairs={{0,4},{1,5},{2,6},{3,7},{4,0},{5,1},{6,2},{7,3},{8,12},{9,13},{10,... | collective-permute-start | bytes 350216 | tf_op jit(solution)/shard_map/ppermute | solution.py:1113
  (36 other events, 226.9 us)
Sparse Core Ops, SparseCore 0:
  11.6 95.6 all-gather.2
  129.9 69.6 all-gather.4
  228.0 61.7 reduce-scatter.3
  309.0 39.5 reduce-scatter.5
  351.0 38.1 reduce-scatter.7
where the time goes:
time: 485 us; the launch traced here: 476 us
  Pallas kernels  178 us (37%)
  waiting for transfers between devices  135 us (28%)
  starting transfers between devices  58.2 us (12%)
  other arithmetic  50.1 us (10%)
  local copies, waits for them, and re-layouts  39.2 us (8%)
  between operations  15 us (3%)
    ppermute x36, waiting for transfers between devices, swap(): lax.ppermute(value, axis, [(i, i ^ stride) for i in range(lax.axis_size(a...  94.5 us
    pallas_call x2, Pallas kernels, attend_back(): pl.pallas_call(functools.partial(attend_back_kernel, head_dim, tiles), gr...  45.1 us
    ppermute x36, starting transfers between devices, swap(): lax.ppermute(value, axis, [(i, i ^ stride) for i in range(lax.axis_size(a...  41.5 us
    pallas_call x2, Pallas kernels, attend(): pl.pallas_call(functools.partial(attend_kernel, head_dim, tiles), grid_sp...  37.9 us
    pallas_call x1, Pallas kernels, dec_mid(): pl.pallas_call(functools.partial(dec_mid_kernel, steps, chunks, packed),...  28.2 us
    ppermute x6, waiting for transfers between devices, along_line(): lax.ppermute(value, 'fsdp', [(i, (i + 2 * by) % size) for i in range(size)])  22.1 us
    convert_element_type x18, other arithmetic, term_sum(): return total.astype(kind)  21.4 us
    pallas_call x1, Pallas kernels, enc_mid_back(): pl.pallas_call(functools.partial(enc_mid_back_kernel, chunks, packed), gr...  17.1 us
  transfers between devices with their start and end apart: 47, of which 25 were waited for; matrix products, arithmetic and copies ran while one was open for 15% of the time, Pallas kernels for 31%

commit v1 on v0

--- a/solution.py
+++ b/solution.py
@@ -1360,17 +1360,12 @@
     while one.order:
         one.step()
         two.step()
-    dec_gather = Gather(dec_first, line + dp)
-    one.piece = dec_gather.tie(one.piece)
-    dec_gather.begin()
     enc_all = join([one.piece, two.piece], core)
-    enc_all = dec_gather.end_beside(enc_all)
-    while len(dec_gather.order) > 3:
-        dec_gather.step()
     evecs = enc_all[:, vec_at:].T[:16].astype(F32)
     up_bias = long_vector(evecs[10:14], devices)
     emb_bias = evecs[14].reshape(devices, erows)[:, :drows].reshape(1, -1)
 
+    dec_gather = Gather(dec_first, line + dp)
     enc_all, evecs = dec_gather.tie((enc_all, evecs))
     dec_gather.begin()
     qkv = enc_qkv_call(enc_input, evecs, enc_all)
@@ -1379,6 +1374,8 @@
     dec_gather.begin()
     attended, inverse, weights = attend(qkv, enc_segments, enc_col, HDIM)
     attended = dec_gather.end_beside(attended)
+    while len(dec_gather.order) > 2:
+        dec_gather.step()
     dec_gather.begin()
     mid, enc_out, final, act, slope, embedded, down_w = enc_mid(
         enc_input,
@@ -1394,6 +1391,10 @@
     embedded, dec_rest = dec_gather.end_beside((embedded, dec_rest))
     emb_got = [along_line(embedded, by) for by in range(1, chips)]
     dec_rest = [lax.all_gather(w, AXES, axis=0, tiled=True) for w in dec_rest]
+    dec_gather.begin()
+    emb_got = dec_gather.end_beside(emb_got)
+    emb_own = jnp.stack([embedded] + emb_got)
+    emb_got = swap(emb_own, core)
     dec_got = swap(dec_gather.piece, core)
     dim = dec_got.ndim - 2
     dec_all = pair(dec_gather.piece, dec_got, bit_here(core), dim)
@@ -1401,11 +1402,6 @@
     dvecs = pair(dec_gather.piece[..., dvec_at:], dec_got[..., dvec_at:], bit_here(core), dim)
     dvecs = dvecs.reshape(-1, LANES).T[:16].astype(F32)
     dup_bias = long_vector(dvecs[10:14], devices)
-    emb_got, dec_all, dvecs, dup_bias = lax.optimization_barrier(
-        (emb_got, dec_all, dvecs, dup_bias)
-    )
-    emb_own = jnp.stack([embedded] + emb_got)
-    emb_got = swap(emb_own, core)
     limit = 2 * chips * enc_rows // BLOCK
     dec_in, dqkv = dec_in_call(
         block_order, chip.reshape(1), here, emb_own, emb_got, pos, dvecs, dec_all
@@ -1467,7 +1463,9 @@
 
     emb_back = [along_line(term_sum(piece_of(chip + by), LOW), by) for by in range(1, chips)]
     dec_grads = dec_grad(dec_in, ddq, ddk, ddv, dvecs, dsum)
-    emb_back, dec_grads, dec_own = lax.optimization_barrier((emb_back, dec_grads, dec_own))
+    emb_back[0], dec_grads, dec_own = lax.optimization_barrier(
+        (emb_back[0], dec_grads, dec_own)
+    )
     dec_grads = lax.psum_scatter(dec_grads, "dp", scatter_dimension=0, tiled=True)
     elow = term_sum(piece_of(chip) + emb_back, LOW)
     *ew, eb1, esum_emb, esum_mid, gmid, gatt = enc_mid_back(

time: 485 us -> 491 us (1.012)
  Pallas kernels: 178 us -> 184 us
    reduce_scatter x1, waiting for transfers between devices: 16.1 us -> 0.01 us  [per_device(): lax.psum_scatter(dec_grads, 'dp', scatter_dimension=0, tiled=True)]
    ppermute x6, waiting for transfers between devices: 22.1 us -> 31 us  [along_line(): lax.ppermute(value, 'fsdp', [(i, (i + 2 * by) % size) for i in range(size)])]
  transfers between devices with their start and end apart: 47 -> 47, of which waited for: 25 -> 23; matrix products, arithmetic and copies ran while one was open for 15% -> 16% of each run, Pallas kernels for 31% -> 32%
where the time goes in v1:
time: 491 us; the launch traced here: 482 us
  Pallas kernels  184 us (37%)
  waiting for transfers between devices  132 us (27%)
  starting transfers between devices  58.4 us (12%)
  other arithmetic  52.8 us (11%)
  local copies, waits for them, and re-layouts  38.9 us (8%)
  between operations  15.2 us (3%)
    ppermute x36, waiting for transfers between devices, swap(): lax.ppermute(value, axis, [(i, i ^ stride) for i in range(lax.axis_size(a...  98.7 us
    pallas_call x2, Pallas kernels, attend_back(): pl.pallas_call(functools.partial(attend_back_kernel, head_dim, tiles), gr...  48.5 us
    ppermute x36, starting transfers between devices, swap(): lax.ppermute(value, axis, [(i, i ^ stride) for i in range(lax.axis_size(a...  42.3 us
    pallas_call x2, Pallas kernels, attend(): pl.pallas_call(functools.partial(attend_kernel, head_dim, tiles), grid_sp...  40.6 us
    ppermute x6, waiting for transfers between devices, along_line(): lax.ppermute(value, 'fsdp', [(i, (i + 2 * by) % size) for i in range(size)])  31 us
    pallas_call x1, Pallas kernels, dec_mid(): pl.pallas_call(functools.partial(dec_mid_kernel, steps, chunks, packed),...  28.2 us
    convert_element_type x18, other arithmetic, term_sum(): return total.astype(kind)  21.3 us
    pallas_call x1, Pallas kernels, enc_mid_back(): pl.pallas_call(functools.partial(enc_mid_back_kernel, chunks, packed), gr...  17.3 us
  transfers between devices with their start and end apart: 47, of which 23 were waited for; matrix products, arithmetic and copies ran while one was open for 16% of the time, Pallas kernels for 32%

profile of v1, /device:TPU:0, one launch (start us, length us, event | category | flops | bytes accessed | tf_op | source)
XLA Modules:
  0.0 482.0 jit_solution(13874786396111620481)
XLA Ops:
  12.3 4.1 collective-permute-start
  16.4 8.3 %collective-permute-done = bf16[24,3712]{1,0:T(8,128)(2,1)S(1)} collective-permute-done((bf16[24,3712]{1,0:T(8,128)(2,1)S(1)}, bf16[24,3712]{1,0:T(8,128)(2,1)S(1)}, u32[]{:S(2)}, u32[]{:S(2)}) %collective-permute-start) | collective-permute-done | bytes 178208 | tf_op jit(solution)/shard_map/ppermute | solution.py:1113
  26.0 13.9 %collective-permute-done.1 = bf16[2,24,3712]{2,1,0:T(8,128)(2,1)S(1)} collective-permute-done((bf16[2,24,3712]{2,1,0:T(8,128)(2,1)S(1)}, bf16[2,24,3712]{2,1,0:T(8,128)(2,1)S(1)}, u32[]{:S(2)}, u32[]{:S(2)}) %collective-permute-start.1) | collective-permute-done | bytes 356384 | tf_op jit(solution)/shard_map/ppermute | solution.py:1113
  41.8 8.7 %cosine_select_fusion.pos_ref = f32[1024,512]{1,0:T(8,128)} fusion(f32[512]{0:T(512)S(1)} %fusion.58, pred[512]{0:T(512)(128)(4,1)S(1)} %fusion.53), kind=kLoop, calls=%fused_computation.12 | loop fusion | flops 1048576 | bytes 2099712 | tf_op jit(solution)/shard_map/jit(_where)/select_n | solution.py:1091
  52.0 2.5 collective-permute-done.5
  56.2 5.5 %collective-permute-done.2 = bf16[2,2,24,1792]{3,2,1,0:T(8,128)(2,1)S(1)} collective-permute-done((bf16[2,2,24,1792]{3,2,1,0:T(8,128)(2,1)S(1)}, bf16[2,2,24,1792]{3,2,1,0:T(8,128)(2,1)S(1)}, u32[]{:S(2)}, u32[]{:S(2)}) %collective-permute-start.2) | collective-permute-done | bytes 344096 | tf_op jit(solution)/shard_map/ppermute | solution.py:1113
  63.3 21.4 %collective-permute-done.6 = bf16[2,2,2,24,1920]{4,3,2,1,0:T(8,128)(2,1)S(1)} collective-permute-done((bf16[2,2,2,24,1920]{4,3,2,1,0:T(8,128)(2,1)S(1)}, bf16[2,2,2,24,1920]{4,3,2,1,0:T(8,128)(2,1)S(1)}, u32[]{:S(2)}, u32[]{:S(2)}) %collective-permute-start.6) | collective-permute-done | bytes 737312 | tf_op jit(solution)/shard_map/ppermute | solution.py:1113
  85.1 3.9 collective-permute-done.3
  89.7 2.8 collective-permute-done.4
  94.1 2.1 bitcast_select_fusion
  96.2 2.8 pad_maximum_fusion.w_ref.wo_ref.we_ref
  99.0 2.3 collective-permute-start.8
  102.0 5.2 %enc_qkv.1.q_ref.k_ref.v_ref = bf16[256,2304]{1,0:T(8,128)(2,1)} custom-call(bf16[256,768]{1,0:T(8,128)(2,1)} %x_ref.5, f32[16,768]{1,0:T(8,128)} %copy.83.vec_ref, bf16[768,3712]{1,0:T(8,128)(2,1)} %pad_maximum_fusion.w_ref.wo_ref.we_ref), custom_call_target="tpu_custom_call" | custom-call | flops 1048576 | bytes 65536 | tf_op jit(solution)/shard_map/enc_qkv/pallas_call | solution.py:367
  107.2 2.6 collective-permute-done.8
  110.8 7.1 %attend.2 = (bf16[256,768]{1,0:T(8,128)(2,1)}, f32[256,768]{1,0:T(8,128)}, bf16[3,1,2,128,1024]{4,3,2,1,0:T(8,128)(2,1)}) custom-call(s32[1,256]{1,0:T(1,128)} %seg_ref.7, bf16[256,2304]{1,0:T(8,128)(2,1)} %enc_qkv.1.q_ref.k_ref.v_ref, bf16[256,2304]{1,0:T(8,128)(2,1)} %enc_qkv.1.q_ref.k_ref.v_ref, bf16[256,2304]{1,0:T(8,128)(2,1)} %enc_qkv.1.q_ref.k_ref.v_ref, ...), custom_call_target="tpu_custom_call" | custom-call | flops 1048576 | bytes 65536 | tf_op jit(solution)/shard_map/attend/pallas_call | solution.py:171
  122.1 13.1 %enc_mid.1 = (f32[256,768]{1,0:T(8,128)}, f32[256,768]{1,0:T(8,128)}, bf16[256,768]{1,0:T(8,128)(2,1)}, bf16[256,3072]{1,0:T(8,128)(2,1)}, f32[256,3072]{1,0:T(8...) custom-call(bf16[256,768]{1,0:T(8,128)(2,1)} %x_ref.5, bf16[256,768]{1,0:T(8,128)(2,1)} %get-tuple-element.136.att_ref.o_ref, ...), custom_call_target="tpu_custom_call" | custom-call | flops 1048576 | bytes 65536 | tf_op jit(solution)/shard_map/enc_mid/pallas_call | solution.py:446
  135.6 2.0 collective-permute-start.12
  138.1 3.0 collective-permute-start.14
  141.1 6.5 %collective-permute-done.12 = bf16[256,512]{1,0:T(8,128)(2,1)S(1)} collective-permute-done((bf16[256,512]{1,0:T(8,128)(2,1)}, bf16[256,512]{1,0:T(8,128)(2,1)S(1)}, u32[]{:S(2)}, u32[]{:S(2)}) %collective-permute-start.12) | collective-permute-done | bytes 262176 | tf_op jit(solution)/shard_map/ppermute | solution.py:1160
  147.6 11.8 %collective-permute-done.13 = bf16[256,512]{1,0:T(8,128)(2,1)S(1)} collective-permute-done((bf16[256,512]{1,0:T(8,128)(2,1)}, bf16[256,512]{1,0:T(8,128)(2,1)S(1)}, u32[]{:S(2)}, u32[]{:S(2)}) %collective-permute-start.13) | collective-permute-done | bytes 262176 | tf_op jit(solution)/shard_map/ppermute | solution.py:1160
  166.0 3.0 bitcast_select_fusion.2.w_ref.wo_ref
  170.0 7.6 %dec_in.1 = (f32[1024,512]{1,0:T(8,128)}, bf16[1024,1536]{1,0:T(8,128)(2,1)}) custom-call(s32[1,8]{1,0:T(1,128)} %order_ref.3, s32[1]{0:T(128)} %bitcast.line_ref, s32[1]{0:T(128)} %bitcast.1.core_ref, bf16[4,256,512]{2,1,0:T(8,128)(2,1)} %copy-done, bf16[4,256,512]{2,1,0:T(8,128)(2,1)} %copy-done, bf16[4,256,512]{2,1,0:T(8,128)(2,1)} %copy-done.1, ...), custom_call_target="tpu_custom_call" | custom-call | flops 1048576 | bytes 65536 | tf_op jit(solution)/shard_map/dec_in/pallas_call | solution.py:786
  177.6 33.5 %attend.3 = (bf16[1024,512]{1,0:T(8,128)(2,1)}, f32[1024,512]{1,0:T(8,128)}, bf16[2,4,8,128,2048]{4,3,2,1,0:T(8,128)(2,1)}) custom-call(s32[1,1024]{1,0:T(1,128)} %seg_ref.6, bf16[1024,1536]{1,0:T(8,128)(2,1)} %get-tuple-element.148.q_ref.k_ref.v_ref, bf16[1024,1536]{1,0:T(8,128)(2,1)} %get-tuple-element.148.q_ref.k_ref.v_ref, ...), custom_call_target="tpu_custom_call" | custom-call | flops 1048576 | bytes 65536 | tf_op jit(solution)/shard_map/attend/pallas_call | solution.py:171
  211.1 28.2 %dec_mid.1 = (bf16[1024,512]{1,0:T(8,128)(2,1)}, f32[1024,512]{1,0:T(8,128)}, bf16[1024,512]{1,0:T(8,128)(2,1)}, bf16[512,4608]{1,0:T(8,128)(2,1)}, f32[4,1,512]{2,1,0:T(1,128)}, /*index=5*/f32[8,512]{1,0:T(8,128)}) custom-call(f32[1024,512]{1,0:T(8,128)} %get-tuple-element.147.x_ref, bf16[1024,512]{1,0:T(8,128)(2,1)} %get-tuple-element.149.att_ref.o_ref, ...), custom_call_target="tpu_custom_call" | custom-call | flops 1048576 | bytes 65536 | tf_op jit(solution)/shard_map/dec_mid/pallas_call | solution.py:920
  241.5 40.5 %attend_back.2 = (bf16[1024,512]{1,0:T(8,128)(2,1)}, bf16[1024,512]{1,0:T(8,128)(2,1)}, bf16[1024,512]{1,0:T(8,128)(2,1)}) custom-call(s32[1,1024]{1,0:T(1,128)} %seg_ref.6, bf16[1024,1536]{1,0:T(8,128)(2,1)} %get-tuple-element.148.q_ref.k_ref.v_ref, bf16[1024,1536]{1,0:T(8,128)(2,1)} %get-tuple-element.148.q_ref.k_ref.v_ref, ...), custom_call_target="tpu_custom_call" | custom-call | flops 1048576 | bytes 65536 | tf_op jit(solution)/shard_map/attend_back/pallas_call | solution.py:282
  282.1 8.7 %dec_back.1 = (f32[16,512]{1,0:T(8,128)}, bf16[4,256,512]{2,1,0:T(8,128)(2,1)}, bf16[4,256,512]{2,1,0:T(8,128)(2,1)}) custom-call(s32[1,8]{1,0:T(1,128)} %order_ref.3, s32[1]{0:T(128)} %bitcast.1.core_ref, f32[1024,512]{1,0:T(8,128)} %get-tuple-element.147.x_ref, bf16[1024,512]{1,0:T(8,128)(2,1)} %get-tuple-element.158.dq_ref, ...), custom_call_target="tpu_custom_call" | custom-call | flops 1048576 | bytes 65536 | tf_op jit(solution)/shard_map/dec_back/pallas_call | solution.py:1030
  291.4 2.5 collective-permute-done.17
  295.2 6.0 %collective-permute-start.18 = (bf16[256,512]{1,0:T(8,128)(2,1)S(1)}, bf16[256,512]{1,0:T(8,128)(2,1)S(1)}, u32[]{:S(2)}, u32[]{:S(2)}) collective-permute-start(bf16[256,512]{1,0:T(8,128)(2,1)S(1)} %get-tuple-element.281), channel_id=1, source_target_pairs={{0,2},{1,3},{2,4},{3,5},{4,6},{5,7},{6,0},{7,1},{8,10},{9,11},{10,... | collective-permute-start | bytes 786440 | tf_op jit(solution)/shard_map/ppermute | solution.py:1160
  301.2 6.6 %dec_grad.1 = bf16[512,1664]{1,0:T(8,128)(2,1)} custom-call(f32[1024,512]{1,0:T(8,128)} %get-tuple-element.147.x_ref, bf16[1024,512]{1,0:T(8,128)(2,1)} %get-tuple-element.158.dq_ref, bf16[1024,512]{1,0:T(8,128)(2,1)} %get-tuple-element.159.dk_ref, bf16[1024,512]{1,0:T(8,128)(2,1)} %get-tuple-element.160.dv_ref, f32[16,512]{1,0:T(8,128)} %copy-done.17, ...), custom_call_target="tpu_custom_call" | custom-call | flops 1048576 | bytes 65536 | tf_op jit(solution)/shard_map/dec_grad/pallas_call | solution.py:1073
  308.9 3.2 collective-permute-start.19
  313.1 11.8 %collective-permute-done.19 = bf16[256,512]{1,0:T(8,128)(2,1)S(1)} collective-permute-done((bf16[256,512]{1,0:T(8,128)(2,1)S(1)}, bf16[256,512]{1,0:T(8,128)(2,1)S(1)}, u32[]{:S(2)}, u32[]{:S(2)}) %collective-permute-start.19) | collective-permute-done | bytes 262176 | tf_op jit(solution)/shard_map/ppermute | solution.py:1160
  326.7 17.3 %enc_mid_back.1 = (bf16[16,24,1280]{2,1,0:T(8,128)(2,1)}, bf16[16,24,1280]{2,1,0:T(8,128)(2,1)}, bf16[16,24,3072]{2,1,0:T(8,128)(2,1)}, bf16[16,24,3072]{2,1,0:T...) custom-call(s32[1]{0:T(128)} %bitcast.1.core_ref, ...), custom_call_target="tpu_custom_call" | custom-call | flops 1048576 | bytes 65536 | tf_op jit(solution)/shard_map/enc_mid_back/pallas_call | solution.py:621
  344.1 2.0 copy.95
  348.3 2.3 pad_maximum_fusion.1
  355.7 2.4 fusion.1
  360.4 3.7 collective-permute-start.25
  365.1 5.9 %collective-permute-start.26 = (bf16[2,2,2,24,1280]{4,3,2,1,0:T(8,128)(2,1)}, bf16[2,2,2,24,1280]{4,3,2,1,0:T(8,128)(2,1)}, u32[]{:S(2)}, u32[]{:S(2)}) collective-permute-start(bf16[2,2,2,24,1280]{4,3,2,1,0:T(8,128)(2,1)} %fusion.20), channel_id=1, source_target_pairs={{0,2},{1,3},{2,0},{3,1},{4,6},{5,7},{6,4},{7,5},{8,10},{9,11},{10,... | collective-permute-start | bytes 1474568 | tf_op jit(solution)/shard_map/ppermute | solution.py:1113
  371.1 7.9 %attend_back.3 = (bf16[256,768]{1,0:T(8,128)(2,1)}, bf16[256,768]{1,0:T(8,128)(2,1)}, bf16[256,768]{1,0:T(8,128)(2,1)}) custom-call(s32[1,256]{1,0:T(1,128)} %seg_ref.7, bf16[256,2304]{1,0:T(8,128)(2,1)} %enc_qkv.1.q_ref.k_ref.v_ref, bf16[256,2304]{1,0:T(8,128)(2,1)} %enc_qkv.1.q_ref.k_ref.v_ref, bf16[256,2304]{1,0:T(8,128)(2,1)} %enc_qkv.1.q_ref.k_ref.v_ref, ...), custom_call_target="tpu_custom_call" | custom-call | flops 1048576 | bytes 65536 | tf_op jit(solution)/shard_map/attend_back/pallas_call | solution.py:282
  379.0 6.9 %enc_qkv_back.1 = (bf16[256,768]{1,0:T(8,128)(2,1)}, bf16[16,24,1152]{2,1,0:T(8,128)(2,1)}, bf16[16,24,1280]{2,1,0:T(8,128)(2,1)}, bf16[16,24,1152]{2,1,0:T(8,128)(2,1)}, bf16[16,24,1280]{2,1,0:T(8,128)(2,1)}) custom-call(s32[1]{0:T(128)} %bitcast.1.core_ref, bf16[256,768]{1,0:T(8,128)(2,1)} %x_ref.5, bf16[256,768]{1,0:T(8,128)(2,1)} %get-tuple-element.198.dq_ref, ...), custom_call_target="tpu_custom_call" | custom-call | flops 1048576 | bytes 65536 | tf_op jit(solution)/shard_map/enc_qkv_back/pallas_call | solution.py:727
  389.7 2.1 collective-permute-done.26
  391.8 2.5 reduce-scatter.8.cloned.1.call-done
  404.2 12.6 %collective-permute-done.31 = bf16[2,2,24,1280]{3,2,1,0:T(8,128)(2,1)S(1)} collective-permute-done((bf16[2,2,24,1280]{3,2,1,0:T(8,128)(2,1)S(1)}, bf16[2,2,24,1280]{3,2,1,0:T(8,128)(2,1)S(1)}, u32[]{:S(2)}, u32[]{:S(2)}) %collective-permute-start.31) | collective-permute-done | bytes 245792 | tf_op jit(solution)/shard_map/ppermute | solution.py:1113
  418.9 2.1 fusion.4
  434.4 3.3 collective-permute-done.35
  445.6 2.9 collective-permute-done.36
  454.6 3.1 collective-permute-done.40
  457.7 4.1 collective-permute-done.39
  465.0 5.4 %collective-permute-done.41 = bf16[24,2432]{1,0:T(8,128)(2,1)} collective-permute-done((bf16[24,2432]{1,0:T(8,128)(2,1)}, bf16[24,2432]{1,0:T(8,128)(2,1)}, u32[]{:S(2)}, u32[]{:S(2)}) %collective-permute-start.41) | collective-permute-done | bytes 116768 | tf_op jit(solution)/shard_map/ppermute | solution.py:1113
  (292 shorter events, 99.0 us)
Async XLA Ops:
  7.2 114.9 %all-gather.3.cloned.1.call-start = ((), (), s32[]{:S(2)}) async-start(), calls=%async_computation.3 | async-start | bytes 9732096 | tf_op jit(solution)/shard_map/all_gather | solution.py:1351
  9.0 202.1 %all-gather.5.cloned.1.call-start = ((), (), s32[]{:S(2)}) async-start(), calls=%async_computation.4 | async-start | bytes 4325376 | tf_op jit(solution)/shard_map/all_gather | solution.py:1393
  12.3 12.4 %collective-permute-start = (bf16[24,3712]{1,0:T(8,128)(2,1)S(1)}, bf16[24,3712]{1,0:T(8,128)(2,1)S(1)}, u32[]{:S(2)}, u32[]{:S(2)}) collective-permute-start(bf16[24,3712]{1,0:T(8,128)(2,1)S(1)} %pad_maximum_fusion.3), channel_id=1, source_target_pairs={{0,4},{1,5},{2,6},{3,7},{4,0},{5,1},{6,2},{7,3},{8,12},{9,13},{10,... | collective-permute-start | bytes 534536 | tf_op jit(solution)/shard_map/ppermute | solution.py:1113
  24.9 15.0 %collective-permute-start.1 = (bf16[2,24,3712]{2,1,0:T(8,128)(2,1)S(1)}, bf16[2,24,3712]{2,1,0:T(8,128)(2,1)S(1)}, u32[]{:S(2)}, u32[]{:S(2)}) collective-permute-start(bf16[2,24,3712]{2,1,0:T(8,128)(2,1)S(1)} %broadcast_select_fusion.7), channel_id=1, source_target_pairs={{0,2},{1,3},{2,0},{3,1},{4,6},{5,7},{6,4},{7,5},{8,10},{9,11},{10,... | collective-permute-start | bytes 1069064 | tf_op jit(solution)/shard_map/ppermute | solution.py:1113
  40.2 14.3 %collective-permute-start.5 = (bf16[2,2,24,1920]{3,2,1,0:T(8,128)(2,1)S(1)}, bf16[2,2,24,1920]{3,2,1,0:T(8,128)(2,1)S(1)}, u32[]{:S(2)}, u32[]{:S(2)}) collective-permute-start(bf16[2,2,24,1920]{3,2,1,0:T(8,128)(2,1)S(1)} %slice.174), channel_id=1, source_target_pairs={{0,16},{8,24},{16,0},{24,8},{1,17},{9,25},{17,1},{25,9},{2,18},{10... | collective-permute-start | bytes 1105928 | tf_op jit(solution)/shard_map/ppermute | solution.py:1113
  50.5 11.2 %collective-permute-start.2 = (bf16[2,2,24,1792]{3,2,1,0:T(8,128)(2,1)S(1)}, bf16[2,2,24,1792]{3,2,1,0:T(8,128)(2,1)S(1)}, u32[]{:S(2)}, u32[]{:S(2)}) collective-permute-start(bf16[2,2,24,1792]{3,2,1,0:T(8,128)(2,1)S(1)} %slice.173), channel_id=1, source_target_pairs={{0,8},{8,0},{16,24},{24,16},{1,9},{9,1},{17,25},{25,17},{2,10},{10... | collective-permute-start | bytes 1032200 | tf_op jit(solution)/shard_map/ppermute | solution.py:1113
  54.7 30.0 %collective-permute-start.6 = (bf16[2,2,2,24,1920]{4,3,2,1,0:T(8,128)(2,1)S(1)}, bf16[2,2,2,24,1920]{4,3,2,1,0:T(8,128)(2,1)S(1)}, u32[]{:S(2)}, u32[]{:S(2)}) collective-permute-start(bf16[2,2,2,24,1920]{4,3,2,1,0:T(8,128)(2,1)S(1)} %broadcast_select_fusion.3), channel_id=1, source_target_pairs={{0,8},{8,0},{16,24},{24,16},{1,9},{9,1},{17,25},{25,17},{2,10},{10... | collective-permute-start | bytes 2211848 | tf_op jit(solution)/shard_map/ppermute | solution.py:1113
  61.8 27.1 %collective-permute-start.3 = (bf16[2,2,2,24,1792]{4,3,2,1,0:T(8,128)(2,1)S(1)}, bf16[2,2,2,24,1792]{4,3,2,1,0:T(8,128)(2,1)S(1)}, u32[]{:S(2)}, u32[]{:S(2)}) collective-permute-start(bf16[2,2,2,24,1792]{4,3,2,1,0:T(8,128)(2,1)S(1)} %broadcast_select_fusion.5), channel_id=1, source_target_pairs={{0,16},{8,24},{16,0},{24,8},{1,17},{9,25},{17,1},{25,9},{2,18},{10... | collective-permute-start | bytes 2064392 | tf_op jit(solution)/shard_map/ppermute | solution.py:1113
  85.0 9.1 %collective-permute-start.7 = (bf16[2,2,2,2,24,1920]{5,4,3,2,1,0:T(8,128)(2,1)S(1)}, bf16[2,2,2,2,24,1920]{5,4,3,2,1,0:T(8,128)(2,1)}, u32[]{:S(2)}, u32[]{:S(2)}) collective-permute-start(bf16[2,2,2,2,24,1920]{5,4,3,2,1,0:T(8,128)(2,1)S(1)} %broadcast_select_fusion), channel_id=1, source_target_pairs={{0,1},{1,0},{2,3},{3,2},{4,5},{5,4},{6,7},{7,6},{8,9},{9,8},{10,11... | collective-permute-start | bytes 4423688 | tf_op jit(solution)/shard_map/ppermute | solution.py:1113
  89.1 3.3 collective-permute-start.4
  99.0 10.8 %collective-permute-start.8 = (bf16[16,2176]{1,0:T(8,128)(2,1)S(1)}, bf16[16,2176]{1,0:T(8,128)(2,1)S(1)}, u32[]{:S(2)}, u32[]{:S(2)}) collective-permute-start(bf16[16,2176]{1,0:T(8,128)(2,1)S(1)} %pad_maximum_fusion.4), channel_id=1, source_target_pairs={{0,4},{1,5},{2,6},{3,7},{4,0},{5,1},{6,2},{7,3},{8,12},{9,13},{10,... | collective-permute-start | bytes 208904 | tf_op jit(solution)/shard_map/ppermute | solution.py:1113
  109.9 8.0 %collective-permute-start.9 = (bf16[2,16,2176]{2,1,0:T(8,128)(2,1)S(1)}, bf16[2,16,2176]{2,1,0:T(8,128)(2,1)S(1)}, u32[]{:S(2)}, u32[]{:S(2)}) collective-permute-start(bf16[2,16,2176]{2,1,0:T(8,128)(2,1)S(1)} %broadcast_select_fusion.9), channel_id=1, source_target_pairs={{0,2},{1,3},{2,0},{3,1},{4,6},{5,7},{6,4},{7,5},{8,10},{9,11},{10,... | collective-permute-start | bytes 417800 | tf_op jit(solution)/shard_map/ppermute | solution.py:1113
  118.0 17.1 %collective-permute-start.10 = (bf16[2,2,16,2176]{3,2,1,0:T(8,128)(2,1)S(1)}, bf16[2,2,16,2176]{3,2,1,0:T(8,128)(2,1)S(1)}, u32[]{:S(2)}, u32[]{:S(2)}) collective-permute-start(bf16[2,2,16,2176]{3,2,1,0:T(8,128)(2,1)S(1)} %broadcast_select_fusion.8), channel_id=1, source_target_pairs={{0,16},{8,24},{16,0},{24,8},{1,17},{9,25},{17,1},{25,9},{2,18},{10... | collective-permute-start | bytes 835592 | tf_op jit(solution)/shard_map/ppermute | solution.py:1113
  135.2 24.5 %copy-start.25 = (bf16[256,512]{1,0:T(8,128)(2,1)S(1)}, bf16[256,512]{1,0:T(8,128)(2,1)}, u32[]{:S(2)}) copy-start(bf16[256,512]{1,0:T(8,128)(2,1)} %get-tuple-element.140) | copy-start | bytes 786436
  135.2 173.6 %reduce-scatter.4.cloned.1.call-start = ((), (), s32[]{:S(2)}) async-start(), calls=%async_computation.5 | async-start | bytes 5898240 | tf_op jit(solution)/shard_map/reduce_scatter | solution.py:1427
  135.4 24.0 %collective-permute-start.11 = (bf16[2,2,2,16,2176]{4,3,2,1,0:T(8,128)(2,1)S(1)}, bf16[2,2,2,16,2176]{4,3,2,1,0:T(8,128)(2,1)S(1)}, u32[]{:S(2)}, u32[]{:S(2)}) collective-permute-start(bf16[2,2,2,16,2176]{4,3,2,1,0:T(8,128)(2,1)S(1)} %broadcast_select_fusion.6), channel_id=1, source_target_pairs={{0,8},{8,0},{16,24},{24,16},{1,9},{9,1},{17,25},{25,17},{2,10},{10... | collective-permute-start | bytes 1671176 | tf_op jit(solution)/shard_map/ppermute | solution.py:1113
  135.6 12.0 %collective-permute-start.12 = (bf16[256,512]{1,0:T(8,128)(2,1)}, bf16[256,512]{1,0:T(8,128)(2,1)S(1)}, u32[]{:S(2)}, u32[]{:S(2)}) collective-permute-start(bf16[256,512]{1,0:T(8,128)(2,1)} %get-tuple-element.140), channel_id=1, source_target_pairs={{0,2},{1,3},{2,4},{3,5},{4,6},{5,7},{6,0},{7,1},{8,10},{9,11},{10,... | collective-permute-start | bytes 786440 | tf_op jit(solution)/shard_map/ppermute | solution.py:1160
  137.7 21.7 %collective-permute-start.13 = (bf16[256,512]{1,0:T(8,128)(2,1)}, bf16[256,512]{1,0:T(8,128)(2,1)S(1)}, u32[]{:S(2)}, u32[]{:S(2)}) collective-permute-start(bf16[256,512]{1,0:T(8,128)(2,1)} %get-tuple-element.140), channel_id=1, source_target_pairs={{0,4},{1,5},{2,6},{3,7},{4,0},{5,1},{6,2},{7,3},{8,12},{9,13},{10,... | collective-permute-start | bytes 786440 | tf_op jit(solution)/shard_map/ppermute | solution.py:1160
  138.1 21.3 %collective-permute-start.14 = (bf16[256,512]{1,0:T(8,128)(2,1)}, bf16[256,512]{1,0:T(8,128)(2,1)S(1)}, u32[]{:S(2)}, u32[]{:S(2)}) collective-permute-start(bf16[256,512]{1,0:T(8,128)(2,1)} %get-tuple-element.140), channel_id=1, source_target_pairs={{0,6},{1,7},{2,0},{3,1},{4,2},{5,3},{6,4},{7,5},{8,14},{9,15},{10,... | collective-permute-start | bytes 786440 | tf_op jit(solution)/shard_map/ppermute | solution.py:1160
  159.6 3.0 collective-permute-start.16
  159.9 9.2 %collective-permute-start.15 = (bf16[4,256,512]{2,1,0:T(8,128)(2,1)S(1)}, bf16[4,256,512]{2,1,0:T(8,128)(2,1)S(1)}, u32[]{:S(2)}, u32[]{:S(2)}) collective-permute-start(bf16[4,256,512]{2,1,0:T(8,128)(2,1)S(1)} %pad_maximum_fusion.2.own_one.own_two), channel_id=1, source_target_pairs={{0,1},{1,0},{2,3},{3,2},{4,5},{5,4},{6,7},{7,6},{8,9},{9,8},{10,11... | collective-permute-start | bytes 3145736 | tf_op jit(solution)/shard_map/ppermute | solution.py:1113
  239.3 109.0 %reduce-scatter.6.cloned.1.call-start = ((), (), s32[]{:S(2)}) async-start(), calls=%async_computation.6 | async-start | bytes 2129920 | tf_op jit(solution)/shard_map/reduce_scatter | solution.py:1469
  290.8 3.1 collective-permute-start.17
  295.2 13.6 %collective-permute-start.18 = (bf16[256,512]{1,0:T(8,128)(2,1)S(1)}, bf16[256,512]{1,0:T(8,128)(2,1)S(1)}, u32[]{:S(2)}, u32[]{:S(2)}) collective-permute-start(bf16[256,512]{1,0:T(8,128)(2,1)S(1)} %get-tuple-element.281), channel_id=1, source_target_pairs={{0,2},{1,3},{2,4},{3,5},{4,6},{5,7},{6,0},{7,1},{8,10},{9,11},{10,... | collective-permute-start | bytes 786440 | tf_op jit(solution)/shard_map/ppermute | solution.py:1160
  308.8 85.5 %reduce-scatter.8.cloned.1.call-start = ((), (), s32[]{:S(2)}) async-start(), calls=%async_computation.7 | async-start | bytes 1806336 | tf_op jit(solution)/shard_map/reduce_scatter | solution.py:1490
  308.9 16.0 %collective-permute-start.19 = (bf16[256,512]{1,0:T(8,128)(2,1)S(1)}, bf16[256,512]{1,0:T(8,128)(2,1)S(1)}, u32[]{:S(2)}, u32[]{:S(2)}) collective-permute-start(bf16[256,512]{1,0:T(8,128)(2,1)S(1)} %get-tuple-element.283), channel_id=1, source_target_pairs={{0,4},{1,5},{2,6},{3,7},{4,0},{5,1},{6,2},{7,3},{8,12},{9,13},{10,... | collective-permute-start | bytes 786440 | tf_op jit(solution)/shard_map/ppermute | solution.py:1160
  312.1 12.8 %collective-permute-start.20 = (bf16[256,512]{1,0:T(8,128)(2,1)S(1)}, bf16[256,512]{1,0:T(8,128)(2,1)S(1)}, u32[]{:S(2)}, u32[]{:S(2)}) collective-permute-start(bf16[256,512]{1,0:T(8,128)(2,1)S(1)} %get-tuple-element.282), channel_id=1, source_target_pairs={{0,6},{1,7},{2,0},{3,1},{4,2},{5,3},{6,4},{7,5},{8,14},{9,15},{10,... | collective-permute-start | bytes 786440 | tf_op jit(solution)/shard_map/ppermute | solution.py:1160
  346.1 9.6 %collective-permute-start.21 = (bf16[2,2,2,2,24,3072]{5,4,2,3,1,0:T(8,128)(2,1)S(1)}, bf16[2,2,2,2,24,3072]{5,4,2,3,1,0:T(8,128)(2,1)}, u32[]{:S(2)}, u32[]{:S(2)}) collective-permute-start(bf16[2,2,2,2,24,3072]{5,4,2,3,1,0:T(8,128)(2,1)S(1)} %copy.95), channel_id=1, source_target_pairs={{0,1},{1,0},{2,3},{3,2},{4,5},{5,4},{6,7},{7,6},{8,9},{9,8},{10,11... | collective-permute-start | bytes 7077896 | tf_op jit(solution)/shard_map/ppermute | solution.py:1113
  348.1 7.6 %collective-permute-start.22 = (bf16[2,2,2,2,24,3072]{5,4,2,3,1,0:T(8,128)(2,1)}, bf16[2,2,2,2,24,3072]{5,4,2,3,1,0:T(8,128)(2,1)}, u32[]{:S(2)}, u32[]{:S(2)}) collective-permute-start(bf16[2,2,2,2,24,3072]{5,4,2,3,1,0:T(8,128)(2,1)} %copy.96), channel_id=1, source_target_pairs={{0,1},{1,0},{2,3},{3,2},{4,5},{5,4},{6,7},{7,6},{8,9},{9,8},{10,11... | collective-permute-start | bytes 7077896 | tf_op jit(solution)/shard_map/ppermute | solution.py:1113
  350.7 5.0 %collective-permute-start.23 = (bf16[2,2,2,2,24,1280]{5,4,3,2,1,0:T(8,128)(2,1)}, bf16[2,2,2,2,24,1280]{5,4,3,2,1,0:T(8,128)(2,1)S(1)}, u32[]{:S(2)}, u32[]{:S(2)}) collective-permute-start(bf16[2,2,2,2,24,1280]{5,4,3,2,1,0:T(8,128)(2,1)} %bitcast.240), channel_id=1, source_target_pairs={{0,1},{1,0},{2,3},{3,2},{4,5},{5,4},{6,7},{7,6},{8,9},{9,8},{10,11... | collective-permute-start | bytes 2949128 | tf_op jit(solution)/shard_map/ppermute | solution.py:1113
  360.3 31.5 %collective-permute-start.24 = (bf16[2,2,2,24,3072]{4,3,1,2,0:T(8,128)(2,1)S(1)}, bf16[2,2,2,24,3072]{4,3,1,2,0:T(8,128)(2,1)S(1)}, u32[]{:S(2)}, u32[]{:S(2)}) collective-permute-start(bf16[2,2,2,24,3072]{4,3,1,2,0:T(8,128)(2,1)S(1)} %fusion), channel_id=1, source_target_pairs={{0,16},{8,24},{16,0},{24,8},{1,17},{9,25},{17,1},{25,9},{2,18},{10... | collective-permute-start | bytes 3538952 | tf_op jit(solution)/shard_map/ppermute | solution.py:1113
  360.4 31.4 %collective-permute-start.25 = (bf16[2,2,2,24,3072]{4,3,1,2,0:T(8,128)(2,1)S(1)}, bf16[2,2,2,24,3072]{4,3,1,2,0:T(8,128)(2,1)}, u32[]{:S(2)}, u32[]{:S(2)}) collective-permute-start(bf16[2,2,2,24,3072]{4,3,1,2,0:T(8,128)(2,1)S(1)} %fusion.1), channel_id=1, source_target_pairs={{0,8},{8,0},{16,24},{24,16},{1,9},{9,1},{17,25},{25,17},{2,10},{10... | collective-permute-start | bytes 3538952 | tf_op jit(solution)/shard_map/ppermute | solution.py:1113
  365.1 26.7 %collective-permute-start.26 = (bf16[2,2,2,24,1280]{4,3,2,1,0:T(8,128)(2,1)}, bf16[2,2,2,24,1280]{4,3,2,1,0:T(8,128)(2,1)}, u32[]{:S(2)}, u32[]{:S(2)}) collective-permute-start(bf16[2,2,2,24,1280]{4,3,2,1,0:T(8,128)(2,1)} %fusion.20), channel_id=1, source_target_pairs={{0,2},{1,3},{2,0},{3,1},{4,6},{5,7},{6,4},{7,5},{8,10},{9,11},{10,... | collective-permute-start | bytes 1474568 | tf_op jit(solution)/shard_map/ppermute | solution.py:1113
  395.9 21.0 %collective-permute-start.30 = (bf16[2,2,24,3072]{3,2,0,1:T(8,128)(2,1)S(1)}, bf16[2,2,24,3072]{3,2,0,1:T(8,128)(2,1)S(1)}, u32[]{:S(2)}, u32[]{:S(2)}) collective-permute-start(bf16[2,2,24,3072]{3,2,0,1:T(8,128)(2,1)S(1)} %fusion.6), channel_id=1, source_target_pairs={{0,16},{8,24},{16,0},{24,8},{1,17},{9,25},{17,1},{25,9},{2,18},{10... | collective-permute-start | bytes 1769480 | tf_op jit(solution)/shard_map/ppermute | solution.py:1113
  397.5 19.4 %collective-permute-start.28 = (bf16[2,2,2,2,24,1280]{5,4,2,3,1,0:T(8,128)(2,1)S(1)}, bf16[2,2,2,2,24,1280]{5,4,2,3,1,0:T(8,128)(2,1)S(1)}, u32[]{:S(2)}, u32[]{:S(2)}) collective-permute-start(bf16[2,2,2,2,24,1280]{5,4,2,3,1,0:T(8,128)(2,1)S(1)} %copy.102), channel_id=1, source_target_pairs={{0,1},{1,0},{2,3},{3,2},{4,5},{5,4},{6,7},{7,6},{8,9},{9,8},{10,11... | collective-permute-start | bytes 2949128 | tf_op jit(solution)/shard_map/ppermute | solution.py:1113
  399.0 17.9 %collective-permute-start.29 = (bf16[2,2,24,3072]{3,2,0,1:T(8,128)(2,1)S(1)}, bf16[2,2,24,3072]{3,2,0,1:T(8,128)(2,1)S(1)}, u32[]{:S(2)}, u32[]{:S(2)}) collective-permute-start(bf16[2,2,24,3072]{3,2,0,1:T(8,128)(2,1)S(1)} %fusion.7), channel_id=1, source_target_pairs={{0,8},{8,0},{16,24},{24,16},{1,9},{9,1},{17,25},{25,17},{2,10},{10... | collective-permute-start | bytes 1769480 | tf_op jit(solution)/shard_map/ppermute | solution.py:1113
  400.9 16.0 %collective-permute-start.27 = (bf16[2,2,2,2,24,1152]{5,4,2,3,1,0:T(8,128)(2,1)S(1)}, bf16[2,2,2,2,24,1152]{5,4,2,3,1,0:T(8,128)(2,1)S(1)}, u32[]{:S(2)}, u32[]{:S(2)}) collective-permute-start(bf16[2,2,2,2,24,1152]{5,4,2,3,1,0:T(8,128)(2,1)S(1)} %copy.101), channel_id=1, source_target_pairs={{0,1},{1,0},{2,3},{3,2},{4,5},{5,4},{6,7},{7,6},{8,9},{9,8},{10,11... | collective-permute-start | bytes 2654216 | tf_op jit(solution)/shard_map/ppermute | solution.py:1113
  402.5 14.4 %collective-permute-start.31 = (bf16[2,2,24,1280]{3,2,1,0:T(8,128)(2,1)S(1)}, bf16[2,2,24,1280]{3,2,1,0:T(8,128)(2,1)S(1)}, u32[]{:S(2)}, u32[]{:S(2)}) collective-permute-start(bf16[2,2,24,1280]{3,2,1,0:T(8,128)(2,1)S(1)} %fusion.24), channel_id=1, source_target_pairs={{0,4},{1,5},{2,6},{3,7},{4,0},{5,1},{6,2},{7,3},{8,12},{9,13},{10,... | collective-permute-start | bytes 737288 | tf_op jit(solution)/shard_map/ppermute | solution.py:1113
  421.9 15.8 %collective-permute-start.34 = (bf16[2,24,6144]{2,1,0:T(8,128)(2,1)}, bf16[2,24,6144]{2,1,0:T(8,128)(2,1)S(1)}, u32[]{:S(2)}, u32[]{:S(2)}) collective-permute-start(bf16[2,24,6144]{2,1,0:T(8,128)(2,1)} %fusion.8), channel_id=1, source_target_pairs={{0,2},{1,3},{2,0},{3,1},{4,6},{5,7},{6,4},{7,5},{8,10},{9,11},{10,... | collective-permute-start | bytes 1769480 | tf_op jit(solution)/shard_map/ppermute | solution.py:1113
  421.9 15.8 %collective-permute-start.33 = (bf16[2,2,2,24,1280]{4,3,1,2,0:T(8,128)(2,1)}, bf16[2,2,2,24,1280]{4,3,1,2,0:T(8,128)(2,1)}, u32[]{:S(2)}, u32[]{:S(2)}) collective-permute-start(bf16[2,2,2,24,1280]{4,3,1,2,0:T(8,128)(2,1)} %fusion.21), channel_id=1, source_target_pairs={{0,8},{8,0},{16,24},{24,16},{1,9},{9,1},{17,25},{25,17},{2,10},{10... | collective-permute-start | bytes 1474568 | tf_op jit(solution)/shard_map/ppermute | solution.py:1113
  423.6 14.1 %collective-permute-start.32 = (bf16[2,2,2,24,1152]{4,3,1,2,0:T(8,128)(2,1)}, bf16[2,2,2,24,1152]{4,3,1,2,0:T(8,128)(2,1)}, u32[]{:S(2)}, u32[]{:S(2)}) collective-permute-start(bf16[2,2,2,24,1152]{4,3,1,2,0:T(8,128)(2,1)} %fusion.27), channel_id=1, source_target_pairs={{0,16},{8,24},{16,0},{24,8},{1,17},{9,25},{17,1},{25,9},{2,18},{10... | collective-permute-start | bytes 1327112 | tf_op jit(solution)/shard_map/ppermute | solution.py:1113
  425.9 11.8 %collective-permute-start.35 = (bf16[2,24,1280]{2,1,0:T(8,128)(2,1)}, bf16[2,24,1280]{2,1,0:T(8,128)(2,1)}, u32[]{:S(2)}, u32[]{:S(2)}) collective-permute-start(bf16[2,24,1280]{2,1,0:T(8,128)(2,1)} %fusion.33), channel_id=1, source_target_pairs={{0,16},{8,24},{16,0},{24,8},{1,17},{9,25},{17,1},{25,9},{2,18},{10... | collective-permute-start | bytes 368648 | tf_op jit(solution)/shard_map/ppermute | solution.py:1113
  438.9 6.6 %collective-permute-start.38 = (bf16[24,1280]{1,0:T(8,128)(2,1)S(1)}, bf16[24,1280]{1,0:T(8,128)(2,1)S(1)}, u32[]{:S(2)}, u32[]{:S(2)}) collective-permute-start(bf16[24,1280]{1,0:T(8,128)(2,1)S(1)} %fusion.44), channel_id=1, source_target_pairs={{0,8},{8,0},{16,24},{24,16},{1,9},{9,1},{17,25},{25,17},{2,10},{10... | collective-permute-start | bytes 184328 | tf_op jit(solution)/shard_map/ppermute | solution.py:1113
  440.6 7.8 %collective-permute-start.37 = (bf16[2,2,24,1280]{3,2,0,1:T(8,128)(2,1)S(1)}, bf16[2,2,24,1280]{3,2,0,1:T(8,128)(2,1)S(1)}, u32[]{:S(2)}, u32[]{:S(2)}) collective-permute-start(bf16[2,2,24,1280]{3,2,0,1:T(8,128)(2,1)S(1)} %fusion.23), channel_id=1, source_target_pairs={{0,16},{8,24},{16,0},{24,8},{1,17},{9,25},{17,1},{25,9},{2,18},{10... | collective-permute-start | bytes 737288 | tf_op jit(solution)/shard_map/ppermute | solution.py:1113
  442.4 6.0 %collective-permute-start.36 = (bf16[2,2,24,1152]{3,2,0,1:T(8,128)(2,1)S(1)}, bf16[2,2,24,1152]{3,2,0,1:T(8,128)(2,1)S(1)}, u32[]{:S(2)}, u32[]{:S(2)}) collective-permute-start(bf16[2,2,24,1152]{3,2,0,1:T(8,128)(2,1)S(1)} %fusion.28), channel_id=1, source_target_pairs={{0,8},{8,0},{16,24},{24,16},{1,9},{9,1},{17,25},{25,17},{2,10},{10... | collective-permute-start | bytes 663560 | tf_op jit(solution)/shard_map/ppermute | solution.py:1113
  444.1 13.6 %collective-permute-start.40 = (bf16[24,6144]{1,0:T(8,128)(2,1)S(1)}, bf16[24,6144]{1,0:T(8,128)(2,1)S(1)}, u32[]{:S(2)}, u32[]{:S(2)}) collective-permute-start(bf16[24,6144]{1,0:T(8,128)(2,1)S(1)} %fusion.16), channel_id=1, source_target_pairs={{0,4},{1,5},{2,6},{3,7},{4,0},{5,1},{6,2},{7,3},{8,12},{9,13},{10,... | collective-permute-start | bytes 884744 | tf_op jit(solution)/shard_map/ppermute | solution.py:1113
  450.8 11.0 %collective-permute-start.39 = (bf16[2,24,2432]{2,1,0:T(8,128)(2,1)S(1)}, bf16[2,24,2432]{2,1,0:T(8,128)(2,1)S(1)}, u32[]{:S(2)}, u32[]{:S(2)}) collective-permute-start(bf16[2,24,2432]{2,1,0:T(8,128)(2,1)S(1)} %fusion.34), channel_id=1, source_target_pairs={{0,2},{1,3},{2,0},{3,1},{4,6},{5,7},{6,4},{7,5},{8,10},{9,11},{10,... | collective-permute-start | bytes 700424 | tf_op jit(solution)/shard_map/ppermute | solution.py:1113
  462.5 8.0 %collective-permute-start.41 = (bf16[24,2432]{1,0:T(8,128)(2,1)}, bf16[24,2432]{1,0:T(8,128)(2,1)}, u32[]{:S(2)}, u32[]{:S(2)}) collective-permute-start(bf16[24,2432]{1,0:T(8,128)(2,1)} %fusion.38), channel_id=1, source_target_pairs={{0,4},{1,5},{2,6},{3,7},{4,0},{5,1},{6,2},{7,3},{8,12},{9,13},{10,... | collective-permute-start | bytes 350216 | tf_op jit(solution)/shard_map/ppermute | solution.py:1113
  (40 other events, 234.9 us)
Sparse Core Ops, SparseCore 0:
  11.6 100.7 all-gather.2
  135.3 67.9 all-gather.4
  239.5 61.9 reduce-scatter.3
  308.9 33.4 reduce-scatter.5
  350.8 43.4 reduce-scatter.7
